TPU v7x, 128 devices: a whole 4x4x4 slice. The times are simulated.
128 devices in a mesh: grp: 2 (over core), dev: 64 (over y, x, z).
Axes of the slice: x: 4, y: 4, z: 4, core: 2. Of those that a mesh axis runs over, the one named last changes fastest.
Arguments:
- queries: bfloat16 [4096, 2048], P(('grp', 'dev')), may hold values from -400 to 400
- keys: bfloat16 [2048, 64, 2048], P(('grp', 'dev')), may hold values from -9 to 9
- values: bfloat16 [2048, 64, 2048], P(('grp', 'dev')), may hold values from -24 to 24
- counts: int32 [256], P(('grp', 'dev')), may hold values from 4 to 28, as said below
- passage_ids: int32 [256, 28], P(('grp', 'dev')), may hold values from 0 to 1023, as said below
- out_weight: bfloat16 [2048, 2048], P('grp'), may hold values from -0.125 to 0.125
Outputs:
- projected: bfloat16 [4096, 2048], P(('grp', 'dev'))
Inputs may be any that keep to these rules, and one draw needn't show every extreme that they name: counts[n] is the number of live entries at the head of row n of passage_ids. `passage_ids`: an id i names passage row i % 16 of device i // 16 along dev in the question's group; the live ids of one question are distinct, entries past counts[n] are ignored. At most one of a device's questions has live passages on any one device of its group, and at most 2 live passages of one question lie on one device; in every draw some device holds live passages of exactly one question of every device of its group, and some question has 2 live passages on one device.
All inputs are finite; a program needn't handle non-finite values.
Results may differ from a plain program's by a relative error of at most 0.012.
Values may be sent and summed in bfloat16 or wider, within the bound.
A program may use at most 192 MiB of HBM per device.

v0:
```python
import math

import jax
import jax.numpy as jnp
from jax import lax
from jax.sharding import PartitionSpec as P

H = 32
HD = 64


NEG_FLOOR = -1e30


def on_device(queries, keys, values, counts, passage_ids, out_weight):
    owner_count = lax.axis_size("dev")
    question_count = counts.shape[0]
    draft_len = queries.shape[0] // question_count
    model_width = queries.shape[1]
    shard_slots = keys.shape[0]
    passage_len = keys.shape[1]
    list_len = passage_ids.shape[1]
    lane_count = question_count // 2
    spread = min(list_len // 2, owner_count // 2)
    per_owner = (list_len + spread - 1) // spread
    scale_factor = 1.0 / math.sqrt(HD)
    highest = lax.Precision.HIGHEST
    holder = passage_ids // shard_slots
    slot_row = passage_ids % shard_slots
    live_mask = jnp.arange(list_len)[None, :] < counts[:, None]
    owner_ids = jnp.arange(owner_count)
    on_owner = live_mask[:, None, :] & (holder[:, None, :] == owner_ids[None, :, None])
    touched = jnp.any(on_owner, axis=2)
    lane_slot = jnp.cumsum(touched.astype(jnp.int32), axis=0) - 1
    lane_ids = jnp.arange(lane_count)
    chosen = jnp.transpose(
        touched[:, :, None] & (lane_slot[:, :, None] == lane_ids[None, None, :]), (1, 2, 0)
    )
    order_rank = jnp.cumsum(on_owner.astype(jnp.int32), axis=2) - 1
    position = on_owner[..., None] & (order_rank[..., None] == jnp.arange(per_owner))
    wanted = jnp.sum(jnp.where(position, slot_row[:, None, :, None], 0), axis=2)
    present = jnp.any(position, axis=2)
    wanted = jnp.where(present, wanted, -1)
    routed_code = jnp.sum(
        jnp.where(chosen[..., None], jnp.transpose(wanted, (1, 0, 2))[:, None, :, :], 0), axis=2
    )
    filled = jnp.any(chosen, axis=2)
    routed_code = jnp.where(filled[..., None], routed_code, -1)
    query_rows = queries.reshape(question_count, draft_len * model_width)
    routed_rows = jnp.einsum(
        "tcq,qr->tcr", chosen.astype(jnp.bfloat16), query_rows, preferred_element_type=jnp.float32
    )
    routed_rows = routed_rows.astype(jnp.bfloat16).reshape(
        owner_count, lane_count, draft_len, model_width
    )
    incoming, incoming_code = (
        lax.all_to_all(routed_rows, "dev", split_axis=0, concat_axis=0, tiled=True),
        lax.all_to_all(routed_code, "dev", split_axis=0, concat_axis=0, tiled=True),
    )
    slot_total = owner_count * lane_count
    slot_block = math.gcd(slot_total, 8)
    block_count = slot_total // slot_block
    stored_len = per_owner * passage_len

    def partial_block(packed):
        query_block, code_block = packed
        usable = code_block >= 0
        gather_rows = jnp.maximum(code_block, 0)
        key_block = keys[gather_rows].reshape(slot_block, stored_len, H, HD)
        value_block = values[gather_rows].reshape(slot_block, per_owner, passage_len, H, HD)
        query_heads = query_block.reshape(slot_block, draft_len, H, HD)
        scores = (
            jnp.einsum(
                "bahd,bshd->bhas", query_heads, key_block, preferred_element_type=jnp.float32
            )
            * scale_factor
        )
        split_scores = scores.reshape(slot_block, H, draft_len, per_owner, passage_len)
        peak_scores = jnp.max(split_scores, axis=-1)
        weights = jnp.exp(split_scores - peak_scores[..., None])
        totals = jnp.sum(weights, axis=-1)
        partial_out = jnp.einsum(
            "bhajt,bjthd->bjahd",
            weights.astype(jnp.bfloat16),
            value_block,
            preferred_element_type=jnp.float32,
        )
        usable_mask = usable[:, None, None, :]
        peak_scores = jnp.where(usable_mask, peak_scores, NEG_FLOOR)
        totals = jnp.where(usable_mask, totals, 0.0)
        stats_peak = jnp.transpose(peak_scores, (0, 3, 1, 2)).reshape(
            slot_block, per_owner, H * draft_len
        )
        stats_total = jnp.transpose(totals, (0, 3, 1, 2)).reshape(
            slot_block, per_owner, H * draft_len
        )
        return (
            partial_out.reshape(slot_block, per_owner, draft_len, model_width),
            stats_peak,
            stats_total,
        )

    results = lax.map(
        partial_block,
        (
            incoming.reshape(block_count, slot_block, draft_len, model_width),
            incoming_code.reshape(block_count, slot_block, per_owner),
        ),
    )
    part_out = results[0].reshape(owner_count, lane_count, per_owner, draft_len, model_width)
    part_peak = results[1].reshape(owner_count, lane_count, per_owner, H * draft_len)
    part_total = results[2].reshape(owner_count, lane_count, per_owner, H * draft_len)
    back_out, back_peak, back_total = (
        lax.all_to_all(part_out, "dev", split_axis=0, concat_axis=0, tiled=True),
        lax.all_to_all(part_peak, "dev", split_axis=0, concat_axis=0, tiled=True),
        lax.all_to_all(part_total, "dev", split_axis=0, concat_axis=0, tiled=True),
    )
    select = chosen[:, :, :, None, None]
    head_peak = jnp.max(jnp.where(select, back_peak[:, :, None], NEG_FLOOR), axis=(0, 1, 3))
    factors = jnp.where(
        select,
        jnp.exp(jnp.minimum(back_peak[:, :, None] - head_peak[None, None, :, None], 0.0)),
        0.0,
    )
    denominator = jnp.sum(factors * back_total[:, :, None], axis=(0, 1, 3))
    numerator = jnp.einsum(
        "tcqjha,tcjahd->qahd",
        factors.reshape(owner_count, lane_count, question_count, per_owner, H, draft_len),
        back_out.reshape(owner_count, lane_count, per_owner, draft_len, H, HD),
        precision=highest,
    )
    head_denominator = jnp.transpose(denominator.reshape(question_count, H, draft_len), (0, 2, 1))
    attended = numerator / head_denominator[..., None]
    attended = attended.astype(jnp.bfloat16).reshape(question_count * draft_len, model_width)
    projected = jnp.dot(
        attended,
        lax.all_gather(out_weight, "grp", axis=0, tiled=True),
        preferred_element_type=jnp.float32,
    )
    return projected.astype(jnp.bfloat16)


def solution(mesh):
    placed = (
        P(("grp", "dev"), None),
        P(("grp", "dev"), None, None),
        P(("grp", "dev"), None, None),
        P(("grp", "dev")),
        P(("grp", "dev"), None),
        P("grp", None),
    )
    return jax.shard_map(
        on_device, mesh=mesh, in_specs=placed, out_specs=P(("grp", "dev"), None), check_vma=False
    )
```

profile of v0, /device:TPU:0, one launch (start us, length us, event | category | flops | bytes accessed | tf_op | source)
XLA Modules:
  0.0 1154.5 jit_solution(4956607672783458626)
XLA Ops:
  9.7 11.5 all-to-all-start
  30.7 7.8 all-to-all-start.1
  38.6 51.9 %all-to-all-done.1 = bf16[64,1,16,2048]{3,2,1,0:T(8,128)(2,1)} async-done(((bf16[64,1,16,2048]{3,2,1,0:T(8,128)(2,1)}), bf16[64,1,16,2048]{3,2,1,0:T(8,128)(2,1)}, u32[]{:S(2)}, u32[]{:S(2)}) %all-to-all-start.1) | async-done | bytes 4194336 | tf_op jit(solution)/shard_map/all_to_all | solution.py:57
  90.5 668.5 %while.14 = (s32[]{:T(128)}, f32[8,8,2,16,2048]{4,3,2,1,0:T(8,128)}, f32[8,8,2,512]{3,1,0,2:T(8,128)S(1)}, f32[8,8,2,512]{3,1,0,2:T(8,128)}, s32[8,8,2]{1,2,0:T(...) while((s32[]{:T(128)}, ...), condition=%wide.region_10.11_spmd, body=%wide.region_7.10_spmd.sunk | while | flops 137364512 | bytes 81072984 | solution.py:103
  104.0 5.0 gather_fusion
  109.0 12.9 %reshape.271 = bf16[8,2,64,32,64]{4,3,2,1,0:T(8,128)(2,1)} reshape(bf16[16,64,2048]{2,1,0:T(8,128)(2,1)} %gather_fusion) | data formatting | bytes 8388608 | tf_op jit(solution)/shard_map/while/body/eval_jaxpr/reshape | solution.py:70
  126.8 12.8 %reshape.272 = bf16[8,128,32,64]{3,2,1,0:T(8,128)(2,1)} reshape(bf16[16,64,2048]{2,1,0:T(8,128)(2,1)} %gather_fusion.1) | data formatting | bytes 8388608 | tf_op jit(solution)/shard_map/while/body/eval_jaxpr/reshape | solution.py:69
  141.8 6.8 fusion.56
  152.3 6.7 reduce_max.21
  160.7 8.5 fusion.57
  172.5 5.0 broadcast_in_dim.163
  185.9 5.0 gather_fusion
  190.9 12.9 %reshape.271 = bf16[8,2,64,32,64]{4,3,2,1,0:T(8,128)(2,1)} reshape(bf16[16,64,2048]{2,1,0:T(8,128)(2,1)} %gather_fusion) | data formatting | bytes 8388608 | tf_op jit(solution)/shard_map/while/body/eval_jaxpr/reshape | solution.py:70
  208.7 12.8 %reshape.272 = bf16[8,128,32,64]{3,2,1,0:T(8,128)(2,1)} reshape(bf16[16,64,2048]{2,1,0:T(8,128)(2,1)} %gather_fusion.1) | data formatting | bytes 8388608 | tf_op jit(solution)/shard_map/while/body/eval_jaxpr/reshape | solution.py:69
  223.7 6.8 fusion.56
  234.1 6.7 reduce_max.21
  242.5 8.5 fusion.57
  254.3 5.0 broadcast_in_dim.163
  267.7 5.0 gather_fusion
  272.7 12.9 %reshape.271 = bf16[8,2,64,32,64]{4,3,2,1,0:T(8,128)(2,1)} reshape(bf16[16,64,2048]{2,1,0:T(8,128)(2,1)} %gather_fusion) | data formatting | bytes 8388608 | tf_op jit(solution)/shard_map/while/body/eval_jaxpr/reshape | solution.py:70
  290.5 12.8 %reshape.272 = bf16[8,128,32,64]{3,2,1,0:T(8,128)(2,1)} reshape(bf16[16,64,2048]{2,1,0:T(8,128)(2,1)} %gather_fusion.1) | data formatting | bytes 8388608 | tf_op jit(solution)/shard_map/while/body/eval_jaxpr/reshape | solution.py:69
  305.5 6.8 fusion.56
  315.9 6.7 reduce_max.21
  324.3 8.5 fusion.57
  336.1 5.0 broadcast_in_dim.163
  349.5 5.0 gather_fusion
  354.5 12.9 %reshape.271 = bf16[8,2,64,32,64]{4,3,2,1,0:T(8,128)(2,1)} reshape(bf16[16,64,2048]{2,1,0:T(8,128)(2,1)} %gather_fusion) | data formatting | bytes 8388608 | tf_op jit(solution)/shard_map/while/body/eval_jaxpr/reshape | solution.py:70
  372.3 12.8 %reshape.272 = bf16[8,128,32,64]{3,2,1,0:T(8,128)(2,1)} reshape(bf16[16,64,2048]{2,1,0:T(8,128)(2,1)} %gather_fusion.1) | data formatting | bytes 8388608 | tf_op jit(solution)/shard_map/while/body/eval_jaxpr/reshape | solution.py:69
  387.3 6.8 fusion.56
  397.8 6.7 reduce_max.21
  406.2 8.5 fusion.57
  418.0 5.0 broadcast_in_dim.163
  436.4 12.9 %reshape.271 = bf16[8,2,64,32,64]{4,3,2,1,0:T(8,128)(2,1)} reshape(bf16[16,64,2048]{2,1,0:T(8,128)(2,1)} %gather_fusion) | data formatting | bytes 8388608 | tf_op jit(solution)/shard_map/while/body/eval_jaxpr/reshape | solution.py:70
  454.2 12.8 %reshape.272 = bf16[8,128,32,64]{3,2,1,0:T(8,128)(2,1)} reshape(bf16[16,64,2048]{2,1,0:T(8,128)(2,1)} %gather_fusion.1) | data formatting | bytes 8388608 | tf_op jit(solution)/shard_map/while/body/eval_jaxpr/reshape | solution.py:69
  469.2 6.8 fusion.56
  479.6 6.7 reduce_max.21
  488.0 8.5 fusion.57
  499.8 5.0 broadcast_in_dim.163
  518.3 12.9 %reshape.271 = bf16[8,2,64,32,64]{4,3,2,1,0:T(8,128)(2,1)} reshape(bf16[16,64,2048]{2,1,0:T(8,128)(2,1)} %gather_fusion) | data formatting | bytes 8388608 | tf_op jit(solution)/shard_map/while/body/eval_jaxpr/reshape | solution.py:70
  536.1 12.8 %reshape.272 = bf16[8,128,32,64]{3,2,1,0:T(8,128)(2,1)} reshape(bf16[16,64,2048]{2,1,0:T(8,128)(2,1)} %gather_fusion.1) | data formatting | bytes 8388608 | tf_op jit(solution)/shard_map/while/body/eval_jaxpr/reshape | solution.py:69
  551.1 6.8 fusion.56
  561.5 6.7 reduce_max.21
  569.9 8.5 fusion.57
  581.7 5.0 broadcast_in_dim.163
  600.1 12.9 %reshape.271 = bf16[8,2,64,32,64]{4,3,2,1,0:T(8,128)(2,1)} reshape(bf16[16,64,2048]{2,1,0:T(8,128)(2,1)} %gather_fusion) | data formatting | bytes 8388608 | tf_op jit(solution)/shard_map/while/body/eval_jaxpr/reshape | solution.py:70
  617.9 12.8 %reshape.272 = bf16[8,128,32,64]{3,2,1,0:T(8,128)(2,1)} reshape(bf16[16,64,2048]{2,1,0:T(8,128)(2,1)} %gather_fusion.1) | data formatting | bytes 8388608 | tf_op jit(solution)/shard_map/while/body/eval_jaxpr/reshape | solution.py:69
  632.9 6.8 fusion.56
  643.3 6.7 reduce_max.21
  651.7 8.5 fusion.57
  663.5 5.0 broadcast_in_dim.163
  681.9 12.9 %reshape.271 = bf16[8,2,64,32,64]{4,3,2,1,0:T(8,128)(2,1)} reshape(bf16[16,64,2048]{2,1,0:T(8,128)(2,1)} %gather_fusion) | data formatting | bytes 8388608 | tf_op jit(solution)/shard_map/while/body/eval_jaxpr/reshape | solution.py:70
  699.7 12.8 %reshape.272 = bf16[8,128,32,64]{3,2,1,0:T(8,128)(2,1)} reshape(bf16[16,64,2048]{2,1,0:T(8,128)(2,1)} %gather_fusion.1) | data formatting | bytes 8388608 | tf_op jit(solution)/shard_map/while/body/eval_jaxpr/reshape | solution.py:69
  714.7 6.8 fusion.56
  725.2 6.7 reduce_max.21
  733.6 8.5 fusion.57
  745.4 5.0 broadcast_in_dim.163
  759.9 11.5 all-to-all-start.3
  772.6 9.4 all-to-all-done.3
  782.0 15.3 %all_to_all.25 = f32[64,1,2,512]{3,2,1,0:T(2,128)S(1)} all-to-all(f32[64,1,2,512]{3,2,1,0:T(2,128)S(1)} %copy.142), channel_id=1, replica_groups=mesh['grp'=2,'dev'=64] {'dev'}, dimensions={0} | all-to-all | bytes 524288 | tf_op jit(solution)/shard_map/all_to_all | solution.py:116
  797.3 5.9 all-to-all-start.2
  805.5 253.7 %all-to-all-done.2 = f32[64,1,2,16,2048]{4,3,2,1,0:T(8,128)} async-done(((f32[64,1,2,16,2048]{4,3,2,1,0:T(8,128)}), f32[64,1,2,16,2048]{4,3,2,1,0:T(8,128)}, u32[]{:S(2)}, u32[]{:S(2)}) %all-to-all-start.2) | async-done | bytes 16777248 | tf_op jit(solution)/shard_map/all_to_all | solution.py:114
  1059.2 27.9 %reshape.229 = f32[64,2,16,32,64]{4,3,2,1,0:T(8,128)} reshape(f32[64,1,2,16,2048]{4,3,2,1,0:T(8,128)} %all-to-all-done.2) | data formatting | bytes 33554432 | tf_op jit(solution)/shard_map/reshape.20
  1087.1 54.2 %fusion.19 = f32[16,32,64,2]{2,3,1,0:T(2,128)S(1)} fusion(f32[64,2,16,32,64]{4,3,2,1,0:T(8,128)} %reshape.229, pred[64,2]{0,1:T(4,128)(4,1)S(1)} %copy-done.2, f32[2,32,16]{0,1,2:T(8,128)S(1)} %copy.138, f32[64,2,32,16]{0,1,2,3:T(2,128)S(1)} %copy.136), kind=kOutput, calls=%fused_computation.28 | convolution fusion | flops 101056512 | bytes 17305728 | tf_op jit(solution)/shard_map/tcqjha,tcjahd->qahd/dot_general | solution.py:126
  1141.8 5.6 convolution_convert_fusion.1
  (241 shorter events, 230.2 us)
Async XLA Ops:
  8.1 19.7 %copy-start.1 = (pred[64,2]{0,1:T(4,128)(4,1)}, pred[64,2]{0,1:T(4,128)(4,1)S(1)}, u32[]{:S(2)}) copy-start(pred[64,2]{0,1:T(4,128)(4,1)S(1)} %fusion.35) | copy-start | bytes 388
  9.7 21.0 %all-to-all-start = ((s32[64,1,2]{2,1,0:T(1,128)}), s32[64,1,2]{2,1,0:T(1,128)S(1)}, u32[]{:S(2)}, u32[]{:S(2)}) async-start(s32[64,1,2]{2,1,0:T(1,128)} %copy.129), calls=%async_computation | async-start | bytes 65536 | tf_op jit(solution)/shard_map/all_to_all | solution.py:58
  30.7 59.8 %all-to-all-start.1 = ((bf16[64,1,16,2048]{3,2,1,0:T(8,128)(2,1)}), bf16[64,1,16,2048]{3,2,1,0:T(8,128)(2,1)}, u32[]{:S(2)}, u32[]{:S(2)}) async-start(bf16[64,1,16,2048]{3,2,1,0:T(8,128)(2,1)} %bitcast.84), calls=%async_computation.1 | async-start | bytes 8388608 | tf_op jit(solution)/shard_map/all_to_all | solution.py:57
  177.5 3.3 copy-start
  259.3 3.3 copy-start
  341.1 3.3 copy-start
  423.0 3.3 copy-start
  504.8 3.4 copy-start
  586.7 3.3 copy-start
  668.5 3.3 copy-start
  750.4 3.3 copy-start
  759.9 22.1 %all-to-all-start.3 = ((f32[64,1,2,512]{3,2,1,0:T(2,128)}), f32[64,1,2,512]{3,2,1,0:T(2,128)S(1)}, u32[]{:S(2)}, u32[]{:S(2)}) async-start(f32[64,1,2,512]{3,2,1,0:T(2,128)} %copy.134), calls=%async_computation.3 | async-start | bytes 524288 | tf_op jit(solution)/shard_map/all_to_all | solution.py:115
  797.3 261.9 %all-to-all-start.2 = ((f32[64,1,2,16,2048]{4,3,2,1,0:T(8,128)}), f32[64,1,2,16,2048]{4,3,2,1,0:T(8,128)}, u32[]{:S(2)}, u32[]{:S(2)}) async-start(f32[64,1,2,16,2048]{4,3,2,1,0:T(8,128)} %bitcast.83), calls=%async_computation.2 | async-start | bytes 33554432 | tf_op jit(solution)/shard_map/all_to_all | solution.py:114
  803.1 0.8 copy-start.2
  803.1 338.7 %all-gather.2.cloned.1.call-start = ((), (), s32[]{:S(2)}) async-start(), calls=%async_computation.5 | async-start | bytes 12582912 | tf_op jit(solution)/shard_map/all_gather | solution.py:137
Sparse Core Ops, SparseCore 0:
  805.6 23.7 all-gather.1
where the time goes:
time: 1170 us; the launch traced here: 1150 us
  local copies, waits for them, and re-layouts  495 us (42%)
  waiting for transfers between devices  319 us (27%)
  matrix products  184 us (16%)
  other arithmetic  76.9 us (7%)
  starting transfers between devices  36.7 us (3%)
  blocking collectives  15.3 us (1%)
  loops' own time  14.2 us (1%)
  between operations  13.8 us (1%)
    all_to_all x1, waiting for transfers between devices, on_device(): lax.all_to_all(part_out, 'dev', split_axis=0, concat_axis=0, tiled=True)  254 us
    reshape x8, local copies, waits for them, and re-layouts, partial_block(): values[gather_rows].reshape(slot_block, per_owner, passage_len, H, HD)  103 us
    reshape x8, local copies, waits for them, and re-layouts, partial_block(): key_block = keys[gather_rows].reshape(slot_block, stored_len, H, HD)  103 us
    dot_general x8, matrix products, partial_block(): jnp.einsum('bhajt,bjthd->bjahd', weights.astype(jnp.bfloat16), value_bloc...  68 us
    dot_general x8, matrix products, partial_block(): jnp.einsum('bahd,bshd->bhas', query_heads, key_block, preferred_element_t...  54.5 us
    dot_general x1, matrix products, on_device(): jnp.einsum('tcqjha,tcjahd->qahd', factors.reshape(owner_count, lane_count...  54.2 us
    reduce_max x8, other arithmetic, partial_block(): peak_scores = jnp.max(split_scores, axis=-1)  53.6 us
    all_to_all x1, waiting for transfers between devices, on_device(): lax.all_to_all(routed_rows, 'dev', split_axis=0, concat_axis=0, tiled=True)  51.9 us
  transfers between devices with their start and end apart: 5, of which 4 were waited for; matrix products, arithmetic and copies ran while one was open for 8% of the time, Pallas kernels for 0%

commit v1 on v0

v1 whole, which is shorter than its diff:
```python
import jax
import jax.numpy as jnp
from jax import lax
from jax.experimental import pallas as pl
from jax.experimental.pallas import tpu as pltpu
from jax.sharding import PartitionSpec as P

D = 2048
H = 32
HD = 64
QT = 16
PT = 64
GW = 256
GH = GW // HD
GROUPS = D // GW
LANE = 128
SIDE = 4
OWNERS = SIDE * SIDE * SIDE
HALVES = 2
HW = D // HALVES
HG = HW // GW
SPIN = 21
BATCH = 8
DEAD = -1e30
WIDE = D + LANE
CUTS = ((0, 384), (384, 384), (768, 256))
ORDERS = (("x", "y", "z"), ("y", "z", "x"), ("z", "x", "y"))
MESH = pl.DeviceIdType.MESH


def torus_kernel(
    ids_ref, mine_ref, k_hbm, v_hbm, w_hbm, out_ref,
    q0_ref, q1_ref, k_ref, v_ref, w_ref, part_ref, back_ref, stat_ref, ask_ref, told_ref, ask_smem, told_smem,
    lse_ref, factor_ref, wide_ref, sum_ref,
    load_sem, home_sem, code_send, code_recv, w_sem, ring_send, ring_recv, part_send, part_recv,
):
    me = lax.axis_index("dev")
    grp = lax.axis_index("grp")
    own = {"y": me // (SIDE * SIDE), "x": lax.rem(me // SIDE, SIDE), "z": lax.rem(me, SIDE)}
    q_refs = (q0_ref, q1_ref)

    def partner(i, sign):
        offset = lax.rem(i * SPIN, OWNERS)
        step = {"y": offset // (SIDE * SIDE), "x": lax.rem(offset // SIDE, SIDE), "z": lax.rem(offset, SIDE)}
        at = {a: lax.rem(own[a] + (step[a] if sign > 0 else SIDE - step[a]), SIDE) for a in own}
        return (at["y"] * SIDE + at["x"]) * SIDE + at["z"]

    def device(axis, at):
        spot = dict(own)
        spot[axis] = at
        return (grp, (spot["y"] * SIDE + spot["x"]) * SIDE + spot["z"])

    def moved(axis, by):
        return lax.rem(own[axis] + by, SIDE)

    loads = [
        pltpu.make_async_copy(k_hbm, k_ref, load_sem.at[0]),
        pltpu.make_async_copy(v_hbm, v_ref, load_sem.at[1]),
    ]
    for load in loads:
        load.start()
    barrier = pltpu.get_barrier_semaphore()

    def greet(i, carry):
        pl.semaphore_signal(barrier, inc=1, device_id=(grp, partner(i, 1)), device_id_type=MESH)
        return carry

    lax.fori_loop(1, OWNERS, greet, 0)
    pl.semaphore_signal(barrier, inc=1, device_id=(1 - grp, me), device_id_type=MESH)

    homes = [
        pltpu.make_async_copy(
            mine_ref.at[:, pl.ds(half * HW, HW)], q_refs[half].at[own["y"], own["x"], own["z"]], home_sem.at[half]
        )
        for half in range(HALVES)
    ]
    for home in homes:
        home.start()
    ids = jnp.broadcast_to(ids_ref[...], (OWNERS, LANE))
    owner_row = lax.broadcasted_iota(jnp.int32, (OWNERS, LANE), 0)
    key = lax.broadcasted_iota(jnp.int32, (OWNERS, LANE), 1) * 16 + (ids & 15)
    here = (ids >> 4) == owner_row
    first = jnp.min(jnp.where(here, key, 1 << 20), axis=1, keepdims=True)
    last = jnp.max(jnp.where(here, key, -1), axis=1, keepdims=True)
    code = jnp.where(last < 0, -1, (first >> 10) + ((first & 15) << 1) + ((last & 15) << 5))
    ask_ref[...] = jnp.broadcast_to(code, (OWNERS, LANE)).reshape(OWNERS, 1, LANE)

    pl.semaphore_wait(barrier, OWNERS)

    def ring_block(half, part, stage, at, rows):
        order = ORDERS[part]
        spot = {axis: own[axis] for axis in order}
        for axis in order[:stage]:
            spot[axis] = pl.ds(0, SIDE)
        spot[order[stage]] = at
        return q_refs[half].at[spot["y"], spot["x"], spot["z"], pl.ds(*rows), pl.ds(*CUTS[part])]

    whole, lower, upper = (0, 2 * QT), (0, QT), (QT, QT)
    both = ((0, 1, lower), (1, SIDE - 1, upper))

    def ring_copy(half, part, stage, kind, at, rows, to, source=None):
        dst = ring_block(half, part, stage, at, rows)
        return pltpu.make_async_remote_copy(
            src_ref=dst if source is None else source,
            dst_ref=dst,
            send_sem=ring_send.at[half, part, stage, kind],
            recv_sem=ring_recv.at[half, part, stage, kind],
            device_id=device(ORDERS[part][stage], to),
            device_id_type=MESH,
        )

    def ring_own(half, part, stage, kind, by):
        axis = ORDERS[part][stage]
        source = None
        if stage == 0:
            source = mine_ref.at[:, pl.ds(half * HW + CUTS[part][0], CUTS[part][1])]
        return ring_copy(half, part, stage, kind, own[axis], whole, moved(axis, by), source)

    def ring_pass(half, part, stage, kind, by, rows):
        axis = ORDERS[part][stage]
        return ring_copy(half, part, stage, 2 + kind, moved(axis, SIDE - by), rows, moved(axis, by))

    def ring_start(half, stage):
        for part in range(3):
            for kind, by, rows in both:
                ring_own(half, part, stage, kind, by).start()

    def ring_forward(half, stage):
        for kind, by, rows in both:
            for part in range(3):
                axis = ORDERS[part][stage]
                came = moved(axis, SIDE - by)
                ring_copy(half, part, stage, kind, came, whole, came).wait_recv()
                ring_pass(half, part, stage, kind, by, rows).start()

    def ring_end(half, stage):
        for part in range(3):
            axis = ORDERS[part][stage]
            for kind, by, rows in both:
                ring_copy(half, part, stage, 2 + kind, moved(axis, 2), rows, moved(axis, by)).wait_recv()

    def ring_sent(half):
        for stage in range(3):
            for part in range(3):
                for kind, by, rows in both:
                    ring_own(half, part, stage, kind, by).wait_send()
                    ring_pass(half, part, stage, kind, by, rows).wait_send()

    def tell(i, sign):
        to, source = partner(i, 1), partner(i, -1)
        return pltpu.make_async_remote_copy(
            src_ref=ask_ref.at[to],
            dst_ref=told_ref.at[me if sign > 0 else source],
            send_sem=code_send.at[i],
            recv_sem=code_recv.at[i],
            device_id=(grp, to),
            device_id_type=MESH,
        )

    def tell_start(i, carry):
        tell(i, 1).start()
        return carry

    def tell_wait(i, carry):
        tell(i, 1).wait_send()
        tell(i, -1).wait_recv()
        return carry

    half_rows = D // 2
    w_home = pltpu.make_async_copy(w_hbm, w_ref.at[pl.ds(grp * half_rows, half_rows)], home_sem.at[2])
    w_give = pltpu.make_async_remote_copy(
        src_ref=w_hbm,
        dst_ref=w_ref.at[pl.ds(grp * half_rows, half_rows)],
        send_sem=w_sem.at[0],
        recv_sem=w_sem.at[1],
        device_id=(1 - grp, me),
        device_id_type=MESH,
    )
    w_take = pltpu.make_async_remote_copy(
        src_ref=w_hbm,
        dst_ref=w_ref.at[pl.ds((1 - grp) * half_rows, half_rows)],
        send_sem=w_sem.at[0],
        recv_sem=w_sem.at[1],
        device_id=(1 - grp, me),
        device_id_type=MESH,
    )

    ring_start(0, 0)
    lax.fori_loop(1, OWNERS, tell_start, 0)
    told_home = pltpu.make_async_copy(ask_ref.at[me], told_ref.at[me], home_sem.at[3])
    told_home.start()
    homes[0].wait()
    ring_forward(0, 0)
    ring_end(0, 0)
    ring_start(0, 1)
    ring_forward(0, 1)
    ring_end(0, 1)
    ring_start(0, 2)
    ask_move = pltpu.make_async_copy(ask_ref, ask_smem, home_sem.at[4])
    ask_move.start()
    told_home.wait()
    lax.fori_loop(1, OWNERS, tell_wait, 0)
    told_move = pltpu.make_async_copy(told_ref, told_smem, home_sem.at[5])
    told_move.start()
    ring_forward(0, 2)
    w_home.start()
    w_give.start()
    for load in loads:
        load.wait()
    homes[1].wait()
    told_move.wait()
    ask_move.wait()
    ring_end(0, 2)
    ring_start(1, 0)

    row_head = lax.broadcasted_iota(jnp.int32, (GH * QT, GW), 0) // QT
    lane_head = lax.broadcasted_iota(jnp.int32, (GH * QT, GW), 1) // HD
    diag = (row_head == lane_head).astype(jnp.float32).astype(jnp.bfloat16)
    stat_lane = lax.broadcasted_iota(jnp.int32, (QT, LANE), 1)
    near = stat_lane < HD

    def answer(half, i, sign):
        cols = pl.ds(0, HW) if half == 0 else pl.ds(HW, WIDE - HW)
        return pltpu.make_async_remote_copy(
            src_ref=part_ref.at[i, :, cols],
            dst_ref=back_ref.at[me if sign > 0 else partner(i, -1), :, cols],
            send_sem=part_send.at[half, i],
            recv_sem=part_recv.at[half, i],
            device_id=(grp, partner(i, 1)),
            device_id_type=MESH,
        )

    def keep():
        return pltpu.make_async_copy(part_ref.at[0], back_ref.at[me], home_sem.at[3])

    def attend(half, b):
        base = b * BATCH
        slots, stats, spots = [], [], []
        for n in range(BATCH):
            s = partner(base + n, 1)
            told = jnp.maximum(told_smem[s, 0, 0], 0)
            slots.append((told & 1, (told >> 1) & 15, (told >> 5) & 15))
            spots.append((s // (SIDE * SIDE), lax.rem(s // SIDE, SIDE), lax.rem(s, SIDE)))
            stats.append(stat_ref[base + n] if half else jnp.zeros((QT, LANE), jnp.float32))
        items = [(n, g) for n in range(BATCH) for g in range(HG)]
        scores, weights = {}, {}

        def score(n, g):
            which, first, second = slots[n]
            near_cols = slice(g * GW, (g + 1) * GW)
            cols = slice(half * HW + g * GW, half * HW + (g + 1) * GW)
            q_ref = q_refs[half]
            q = jnp.where(which > 0, q_ref[(*spots[n], slice(QT, 2 * QT), near_cols)], q_ref[(*spots[n], slice(0, QT), near_cols)])
            lhs = jnp.concatenate([q * jnp.bfloat16(0.125)] * GH, axis=0) * diag
            k = jnp.concatenate([k_ref[first, :, cols], k_ref[second, :, cols]], axis=0)
            scores[n, g] = lax.dot_general(lhs, k, (((1,), (1,)), ((), ())), preferred_element_type=jnp.float32)

        def weigh(n, g):
            which, first, second = slots[n]
            values = scores.pop((n, g))
            peak = jnp.max(values, axis=1, keepdims=True)
            shaped = jnp.exp(values - peak)
            total = jnp.sum(shaped, axis=1, keepdims=True)
            lse = peak + jnp.log(total * jnp.where(first == second, 0.5, 1.0))
            for h in range(GH):
                head = (half * HG + g) * GH + h
                stats[n] = jnp.where(stat_lane % H == head, lse[h * QT : (h + 1) * QT], stats[n])
            weights[n, g] = (shaped.astype(jnp.bfloat16), 1.0 / total)

        def apply(n, g):
            which, first, second = slots[n]
            start = half * HW + g * GW
            cols = slice(start, start + GW)
            shaped, inverse = weights.pop((n, g))
            v = jnp.concatenate([v_ref[first, :, cols], v_ref[second, :, cols]], axis=0)
            full = jnp.dot(shaped, v, preferred_element_type=jnp.float32)
            for t in range(GW // LANE):
                lanes = slice(t * LANE, (t + 1) * LANE)
                a, b = (slice((2 * t + e) * QT, (2 * t + e + 1) * QT) for e in (0, 1))
                part = jnp.where(near, full[a, lanes] * inverse[a], full[b, lanes] * inverse[b])
                part_ref[base + n, :, start + t * LANE : start + (t + 1) * LANE] = part.astype(jnp.bfloat16)

        for at in range(len(items) + 4):
            if at < len(items):
                score(*items[at])
            if 2 <= at < len(items) + 2:
                weigh(*items[at - 2])
            if 4 <= at:
                apply(*items[at - 4])
        for n in range(BATCH):
            if half == 0:
                stat_ref[base + n] = stats[n]
                continue
            high = stats[n].astype(jnp.bfloat16).astype(jnp.float32)
            rest = stats[n] - high
            middle = rest.astype(jnp.bfloat16).astype(jnp.float32)
            low = rest - middle
            pieces = jnp.where(stat_lane < H, high, jnp.where(stat_lane < 2 * H, middle, low))
            part_ref[base + n, :, D:] = jnp.where(stat_lane < 3 * H, pieces, 0.0).astype(jnp.bfloat16)
        for n in range(BATCH):
            if n:
                answer(half, base + n, 1).start()
            else:

                @pl.when(b > 0)
                def _():
                    answer(half, base, 1).start()

    def attend_first(b, carry):
        attend(0, b)
        steps = (
            lambda: ring_forward(1, 0),
            lambda: (ring_end(1, 0), ring_start(1, 1)),
            lambda: ring_forward(1, 1),
            lambda: (ring_end(1, 1), ring_start(1, 2)),
            None,
            lambda: ring_forward(1, 2),
        )
        for at, step in enumerate(steps):
            if step is not None:
                pl.when(b == at)(lambda step=step: (step(), None)[1])
        return carry

    def attend_second(b, carry):
        attend(1, b)
        return carry

    lax.fori_loop(0, OWNERS // BATCH, attend_first, 0)
    ring_end(1, 2)
    lax.fori_loop(0, OWNERS // BATCH, attend_second, 0)
    keep().start()
    ring_sent(0)
    ring_sent(1)
    keep().wait()

    def finish(i, carry):
        for half in range(HALVES):
            answer(half, i, 1).wait_send()
            answer(half, i, -1).wait_recv()
        return carry

    lax.fori_loop(1, OWNERS, finish, 0)

    fold_row = lax.broadcasted_iota(jnp.int32, (LANE, LANE), 0)
    fold_lane = lax.broadcasted_iota(jnp.int32, (LANE, LANE), 1)
    fold = ((fold_row < 3 * H) & (fold_row % H == fold_lane % H)).astype(jnp.float32).astype(jnp.bfloat16)
    lse_ref[...] = jnp.dot(
        back_ref[:, :, D:].reshape(OWNERS * QT, LANE), fold, preferred_element_type=jnp.float32
    ).reshape(OWNERS, QT, LANE)

    def question(o):
        asked = ask_smem[o, 0, 0]
        return jnp.where(asked < 0, -1, asked & 1)

    def highest(o, tops):
        which, lse = question(o), lse_ref[o]
        return tuple(jnp.maximum(top, jnp.where(which == n, lse, DEAD)) for n, top in enumerate(tops))

    bottom = jnp.full((QT, LANE), DEAD, jnp.float32)
    tops = lax.fori_loop(0, OWNERS, highest, (bottom, bottom), unroll=8)

    def weigh_all(o, totals):
        which = question(o)
        factor = jnp.exp(jnp.minimum(lse_ref[o] - jnp.where(which == 1, tops[1], tops[0]), 0.0))
        factor = jnp.where(which < 0, 0.0, factor)
        lse_ref[o] = factor
        return tuple(total + jnp.where(which == n, factor, 0.0) for n, total in enumerate(totals))

    nothing = jnp.zeros((QT, LANE), jnp.float32)
    totals = lax.fori_loop(0, OWNERS, weigh_all, (nothing, nothing), unroll=8)
    shares = tuple(1.0 / total for total in totals)

    def scale(o, carry):
        factor = lse_ref[o] * jnp.where(question(o) == 1, shares[1], shares[0])
        high = factor.astype(jnp.bfloat16).astype(jnp.float32)
        pieces = jnp.where(stat_lane < H, high, jnp.where(stat_lane < 2 * H, factor - high, 0.0))
        factor_ref[o] = pieces.astype(jnp.bfloat16)
        return carry

    lax.fori_loop(0, OWNERS, scale, 0, unroll=8)
    w_home.wait()
    w_give.wait_send()
    w_take.wait_recv()
    sum_ref[...] = jnp.zeros(sum_ref.shape, jnp.float32)
    spread_row = lax.broadcasted_iota(jnp.int32, (LANE, GW), 0)
    spread_lane = lax.broadcasted_iota(jnp.int32, (LANE, GW), 1)

    def project(g, carry):
        cols = pl.ds(pl.multiple_of(g * GW, GW), GW)
        spread = (spread_row < 2 * H) & (spread_row % H == g * GH + spread_lane // HD)
        wide_ref[...] = jnp.dot(
            factor_ref[...].reshape(OWNERS * QT, LANE),
            spread.astype(jnp.float32).astype(jnp.bfloat16),
            preferred_element_type=jnp.float32,
        ).reshape(OWNERS, QT, GW)

        def add(o, sums):
            which = question(o)
            term = wide_ref[o] * back_ref[o, :, cols].astype(jnp.float32)
            return tuple(total + jnp.where(which == n, term, 0.0) for n, total in enumerate(sums))

        empty = jnp.zeros((QT, GW), jnp.float32)
        attended = jnp.concatenate(lax.fori_loop(0, OWNERS, add, (empty, empty), unroll=8), axis=0)
        sum_ref[...] += jnp.dot(attended.astype(jnp.bfloat16), w_ref[cols, :], preferred_element_type=jnp.float32)
        return carry

    lax.fori_loop(0, GROUPS, project, 0)
    out_ref[...] = sum_ref[...].astype(jnp.bfloat16)


def on_device(queries, keys, values, counts, passage_ids, out_weight):
    list_len = passage_ids.shape[1]
    listed = jnp.arange(list_len)[None, :] < counts[:, None]
    ids = jnp.where(listed, passage_ids, -1).astype(jnp.int32)
    ids = jnp.pad(ids, ((0, 0), (0, LANE // 2 - list_len)), constant_values=-1).reshape(1, LANE)
    half_shape = (SIDE, SIDE, SIDE, 2 * QT, HW)
    return pl.pallas_call(
        torus_kernel,
        out_shape=jax.ShapeDtypeStruct((2 * QT, D), jnp.bfloat16),
        in_specs=[pl.BlockSpec(memory_space=pltpu.VMEM)] * 2 + [pl.BlockSpec(memory_space=pl.ANY)] * 3,
        out_specs=pl.BlockSpec(memory_space=pltpu.VMEM),
        scratch_shapes=[
            pltpu.VMEM(half_shape, jnp.bfloat16),
            pltpu.VMEM(half_shape, jnp.bfloat16),
            pltpu.VMEM(keys.shape, jnp.bfloat16),
            pltpu.VMEM(values.shape, jnp.bfloat16),
            pltpu.VMEM((D, D), jnp.bfloat16),
            pltpu.VMEM((OWNERS, QT, WIDE), jnp.bfloat16),
            pltpu.VMEM((OWNERS, QT, WIDE), jnp.bfloat16),
            pltpu.VMEM((OWNERS, QT, LANE), jnp.float32),
            pltpu.VMEM((OWNERS, 1, LANE), jnp.int32),
            pltpu.VMEM((OWNERS, 1, LANE), jnp.int32),
            pltpu.SMEM((OWNERS, 1, LANE), jnp.int32),
            pltpu.SMEM((OWNERS, 1, LANE), jnp.int32),
            pltpu.VMEM((OWNERS, QT, LANE), jnp.float32),
            pltpu.VMEM((OWNERS, QT, LANE), jnp.bfloat16),
            pltpu.VMEM((OWNERS, QT, GW), jnp.float32),
            pltpu.VMEM((2 * QT, D), jnp.float32),
            pltpu.SemaphoreType.DMA((2,)),
            pltpu.SemaphoreType.DMA((6,)),
            pltpu.SemaphoreType.DMA((OWNERS,)),
            pltpu.SemaphoreType.DMA((OWNERS,)),
            pltpu.SemaphoreType.DMA((2,)),
            pltpu.SemaphoreType.DMA((HALVES, 3, 3, 4)),
            pltpu.SemaphoreType.DMA((HALVES, 3, 3, 4)),
            pltpu.SemaphoreType.DMA((HALVES, OWNERS)),
            pltpu.SemaphoreType.DMA((HALVES, OWNERS)),
        ],
        compiler_params=pltpu.CompilerParams(
            vmem_limit_bytes=60 * 2**20, collective_id=0, has_side_effects=True
        ),
        cost_estimate=pl.CostEstimate(flops=40 * 10**9, bytes_accessed=20 * 2**20, transcendentals=4 * 10**6),
        name="torus",
    )(ids, queries, keys, values, out_weight)


def solution(mesh):
    placed = (
        P(("grp", "dev"), None),
        P(("grp", "dev"), None, None),
        P(("grp", "dev"), None, None),
        P(("grp", "dev")),
        P(("grp", "dev"), None),
        P("grp", None),
    )
    return jax.shard_map(
        on_device, mesh=mesh, in_specs=placed, out_specs=P(("grp", "dev"), None), check_vma=False
    )
```

time: 1170 us -> 142 us (0.12); the launches traced: 1150 us -> 140 us
  local copies, waits for them, and re-layouts: 495 us -> 2.17 us
  waiting for transfers between devices: 319 us -> 0 us
  matrix products: 184 us -> 0 us
  Pallas kernels: 0 us -> 137 us
  other arithmetic: 76.9 us -> 0.75 us
  starting transfers between devices: 36.7 us -> 0 us
  blocking collectives: 15.3 us -> 0 us
  loops' own time: 14.2 us -> 0 us
  between operations: 13.8 us -> 0.01 us
    all_to_all x4 -> x0, waiting for transfers between devices: 318 us -> none  [the longest x1 254 us: on_device(): lax.all_to_all(part_out, 'dev', split_axis=0, concat_axis=0, tiled=True)]
    reshape x37 -> x1, local copies, waits for them, and re-layouts: 247 us -> 0.59 us  [on_device(): jnp.pad(ids, ((0, 0), (0, LANE // 2 - list_len)), constant_values=-1)]
    dot_general x19 -> x0, matrix products: 184 us -> none  [the longest x8 68 us: partial_block(): jnp.einsum('bhajt,bjthd->bjahd', weights.astype(jnp.bfloat16), value_bloc...]
    pallas_call x0 -> x1, Pallas kernels: none -> 137 us  [on_device(): pl.pallas_call(torus_kernel, out_shape=jax.ShapeDtypeStruct((2 * QT, D),...]
    gather x16 -> x0, local copies, waits for them, and re-layouts: 79.4 us -> none  [the longest x8 39.8 us: partial_block(): values[gather_rows].reshape(slot_block, per_owner, passage_len, H, HD)]
    reduce_max x9 -> x0, other arithmetic: 53.8 us -> none  [the longest x8 53.6 us: partial_block(): peak_scores = jnp.max(split_scores, axis=-1)]
    broadcast_in_dim x24 -> x0, local copies, waits for them, and re-layouts: 42.4 us -> none  [on_device(): lax.map(partial_block, (incoming.reshape(block_count, slot_block, draft_l...]
    all_to_all x4 -> x0, starting transfers between devices: 36.7 us -> none  [the longest x1 11.5 us: on_device(): lax.all_to_all(part_peak, 'dev', split_axis=0, concat_axis=0, tiled=True)]
  transfers between devices with their start and end apart: 5 -> 0, of which waited for: 4 -> 0; matrix products, arithmetic and copies ran while one was open for 8% -> 0% of each run, Pallas kernels for 0% -> 0%
where the time goes in v1:
time: 142 us; the launch traced here: 140 us
  Pallas kernels  137 us (96%)
  local copies, waits for them, and re-layouts  2.17 us (2%)
    pallas_call x1, Pallas kernels, on_device(): pl.pallas_call(torus_kernel, out_shape=jax.ShapeDtypeStruct((2 * QT, D),...  137 us

profile of v1, /device:TPU:0, one launch (start us, length us, event | category | flops | bytes accessed | tf_op | source)
XLA Modules:
  0.0 139.6 jit_solution(14917692452005203819)
XLA Ops:
  0.0 0.8 compare_select_fusion
  0.8 0.6 reshape.4.ids_ref
  1.4 136.6 %torus.1 = bf16[32,2048]{1,0:T(8,128)(2,1)} custom-call(s32[1,128]{1,0:T(1,128)} %reshape.4.ids_ref, bf16[32,2048]{1,0:T(8,128)(2,1)} %mine_ref.1, bf16[16,64,2048]{2,1,0:T(8,128)(2,1)} %k_hbm.1, bf16[16,64,2048]{2,1,0:T(8,128)(2,1)} %v_hbm.1, bf16[1024,2048]{1,0:T(8,128)(2,1)} %w_hbm.1), custom_call_target="tpu_custom_call" | custom-call | flops 40000000000 | bytes 20971520 | tf_op jit(solution)/shard_map/torus/pallas_call | solution.py:417
  138.0 1.6 %copy.8 = bf16[32,2048]{1,0:T(8,128)(2,1)} copy(bf16[32,2048]{1,0:T(8,128)(2,1)} %torus.1) | data formatting | bytes 262144
  (1 shorter events, 0.0 us)

commit v2 on v1

v2 whole, which is shorter than its diff:
```python
import jax
import jax.numpy as jnp
from jax import lax
from jax.experimental import pallas as pl
from jax.experimental.pallas import tpu as pltpu
from jax.sharding import PartitionSpec as P

D = 2048
H = 32
HD = 64
QT = 16
PT = 64
GW = 256
GH = GW // HD
GROUPS = D // GW
LANE = 128
SIDE = 4
OWNERS = SIDE * SIDE * SIDE
WS = (768, 768, 512)
STARTS = (0, 768, 1536)
BATCH = 8
DEAD = -1e30
CUTS = (
    ((0, 256), (256, 256), (512, 256)),
    ((0, 256), (256, 256), (512, 256)),
    ((0, 256), (256, 128), (384, 128)),
)
ORDERS = (("x", "y", "z"), ("y", "z", "x"), ("z", "x", "y"))
MESH = pl.DeviceIdType.MESH


def torus_kernel(
    ids_ref, mine_ref, k_hbm, v_hbm, w_hbm, out_ref,
    q0_ref, q1_ref, q2_ref, part0_ref, part1_ref, part2_ref, near0_ref, near1_ref, near2_ref,
    mid0_ref, mid1_ref, mid2_ref, next0_ref, next1_ref, next2_ref,
    late0_ref, late1_ref, late2_ref, last0_ref, last1_ref, last2_ref,
    k_ref, v_ref, w_ref, list_ref, code_ref, code_smem, seen_ref, factor_ref, wide_ref, sum_ref,
    load_sem, home_sem, list_send, list_recv, w_sem, ring_send, ring_recv,
    one_send, one_recv, two_send, two_recv, three_send, three_recv,
):
    me = lax.axis_index("dev")
    grp = lax.axis_index("grp")
    own = {"y": me >> 4, "x": (me >> 2) & 3, "z": me & 3}
    stride = {"y": SIDE * SIDE, "x": SIDE, "z": 1}
    line = {
        axis: {by: (grp, me + ((((own[axis] + by) & 3) - own[axis]) * stride[axis])) for by in range(1, SIDE)}
        for axis in own
    }
    q_refs = (q0_ref, q1_ref, q2_ref)
    parts = (part0_ref, part1_ref, part2_ref)
    nears = (near0_ref, near1_ref, near2_ref)
    mids = (mid0_ref, mid1_ref, mid2_ref)
    nexts = (next0_ref, next1_ref, next2_ref)
    lates = (late0_ref, late1_ref, late2_ref)
    lasts = (last0_ref, last1_ref, last2_ref)

    loads = [
        pltpu.make_async_copy(k_hbm, k_ref, load_sem.at[0]),
        pltpu.make_async_copy(v_hbm, v_ref, load_sem.at[1]),
    ]
    for load in loads:
        load.start()
    barrier = pltpu.get_barrier_semaphore()
    for axis in line:
        for by in line[axis]:
            pl.semaphore_signal(barrier, inc=1, device_id=line[axis][by], device_id_type=MESH)
    pl.semaphore_signal(barrier, inc=1, device_id=(1 - grp, me), device_id_type=MESH)
    homes = [
        pltpu.make_async_copy(
            mine_ref.at[:, pl.ds(STARTS[phase], WS[phase])], q_refs[phase].at[0, 0, 0], home_sem.at[phase]
        )
        for phase in range(3)
    ]
    for home in homes:
        home.start()
    list_ref[0, 0, 0] = ids_ref[...]
    pl.semaphore_wait(barrier, 10)

    whole, lower, upper = (0, 2 * QT), (0, QT), (QT, QT)
    both = ((0, 1, 3, lower), (1, 3, 1, upper))

    def ring_block(phase, part, stage, at, rows):
        order = ORDERS[part]
        spot = {axis: 0 for axis in order}
        for axis in order[:stage]:
            spot[axis] = pl.ds(0, SIDE)
        spot[order[stage]] = at
        first, second, third = (spot[axis] for axis in ORDERS[phase])
        return q_refs[phase].at[first, second, third, pl.ds(*rows), pl.ds(*CUTS[phase][part])]

    def ring_own(phase, part, stage, kind, by, at):
        if stage == 0:
            cut = CUTS[phase][part]
            source = mine_ref.at[:, pl.ds(STARTS[phase] + cut[0], cut[1])]
        else:
            source = ring_block(phase, part, stage, 0, whole)
        return pltpu.make_async_remote_copy(
            src_ref=source,
            dst_ref=ring_block(phase, part, stage, at, whole),
            send_sem=ring_send.at[phase, part, stage, kind],
            recv_sem=ring_recv.at[phase, part, stage, kind],
            device_id=line[ORDERS[part][stage]][by],
            device_id_type=MESH,
        )

    def ring_pass(phase, part, stage, kind, by, at, rows):
        return pltpu.make_async_remote_copy(
            src_ref=ring_block(phase, part, stage, at, rows),
            dst_ref=ring_block(phase, part, stage, 2, rows),
            send_sem=ring_send.at[phase, part, stage, 2 + kind],
            recv_sem=ring_recv.at[phase, part, stage, 2 + kind],
            device_id=line[ORDERS[part][stage]][by],
            device_id_type=MESH,
        )

    def ring_start(phase, stage):
        for part in range(3):
            for kind, by, at, rows in both:
                ring_own(phase, part, stage, kind, by, at).start()

    def ring_forward(phase, stage):
        for kind, by, at, rows in both:
            for part in range(3):
                ring_own(phase, part, stage, kind, by, at).wait_recv()
                ring_pass(phase, part, stage, kind, by, at, rows).start()

    def ring_end(phase, stage):
        for part in range(3):
            for kind, by, at, rows in both:
                ring_pass(phase, part, stage, kind, by, at, rows).wait_recv()

    def ring_sent(phase):
        for stage in range(3):
            for part in range(3):
                for kind, by, at, rows in both:
                    ring_own(phase, part, stage, kind, by, at).wait_send()
                    ring_pass(phase, part, stage, kind, by, at, rows).wait_send()

    def list_copy(stage, by):
        order = ("x", "y", "z")
        spot = {axis: 0 for axis in order}
        for axis in order[:stage]:
            spot[axis] = pl.ds(0, SIDE)
        source = list_ref.at[spot["y"], spot["x"], spot["z"]]
        spot[order[stage]] = SIDE - by
        return pltpu.make_async_remote_copy(
            src_ref=source,
            dst_ref=list_ref.at[spot["y"], spot["x"], spot["z"]],
            send_sem=list_send.at[stage, by],
            recv_sem=list_recv.at[stage, by],
            device_id=line[order[stage]][by],
            device_id_type=MESH,
        )

    def list_start(stage):
        for by in range(1, SIDE):
            list_copy(stage, by).start()

    def list_end(stage):
        for by in range(1, SIDE):
            list_copy(stage, by).wait_recv()

    w_rows = D // 2
    w_home = pltpu.make_async_copy(w_hbm, w_ref.at[pl.ds(grp * w_rows, w_rows)], home_sem.at[3])
    w_give = pltpu.make_async_remote_copy(
        src_ref=w_hbm,
        dst_ref=w_ref.at[pl.ds(grp * w_rows, w_rows)],
        send_sem=w_sem.at[0],
        recv_sem=w_sem.at[1],
        device_id=(1 - grp, me),
        device_id_type=MESH,
    )
    w_take = pltpu.make_async_remote_copy(
        src_ref=w_hbm,
        dst_ref=w_ref.at[pl.ds((1 - grp) * w_rows, w_rows)],
        send_sem=w_sem.at[0],
        recv_sem=w_sem.at[1],
        device_id=(1 - grp, me),
        device_id_type=MESH,
    )

    list_start(0)
    ring_start(0, 0)
    for home in homes:
        home.wait()
    list_end(0)
    list_start(1)
    ring_forward(0, 0)
    list_end(1)
    list_start(2)
    ring_end(0, 0)
    ring_start(0, 1)
    ring_forward(0, 1)
    ring_end(0, 1)
    ring_start(0, 2)
    list_end(2)
    ids = list_ref[...].reshape(OWNERS, LANE)
    key = lax.broadcasted_iota(jnp.int32, (OWNERS, LANE), 1) * 16 + (ids & 15)
    here = (ids >> 4) == me
    first = jnp.min(jnp.where(here, key, 1 << 20), axis=1, keepdims=True)
    last = jnp.max(jnp.where(here, key, -1), axis=1, keepdims=True)
    code = jnp.where(last < 0, -1, (first >> 10) + ((first & 15) << 1) + ((last & 15) << 5))
    code_ref[...] = jnp.broadcast_to(code, (OWNERS, LANE)).reshape(OWNERS, 1, LANE)
    code_move = pltpu.make_async_copy(code_ref, code_smem, home_sem.at[4])
    code_move.start()
    ring_forward(0, 2)
    ring_start(1, 0)
    w_home.start()
    w_give.start()
    for load in loads:
        load.wait()
    code_move.wait()
    ring_end(0, 2)
    ring_forward(1, 0)

    row_head = lax.broadcasted_iota(jnp.int32, (GH * QT, GW), 0) // QT
    lane_head = lax.broadcasted_iota(jnp.int32, (GH * QT, GW), 1) // HD
    diag = (row_head == lane_head).astype(jnp.float32).astype(jnp.bfloat16)
    stat_lane = lax.broadcasted_iota(jnp.int32, (QT, LANE), 1)
    near = stat_lane < HD

    def tree(sources, targets, send_sem, recv_sem, phase, stage, by):
        return pltpu.make_async_remote_copy(
            src_ref=sources[phase].at[by],
            dst_ref=targets[phase].at[by - 1],
            send_sem=send_sem.at[phase, by],
            recv_sem=recv_sem.at[phase, by],
            device_id=line[ORDERS[phase][stage]][by],
            device_id_type=MESH,
        )

    def one(phase, by):
        return tree(parts, nears, one_send, one_recv, phase, 0, by)

    def two(phase, by):
        return tree(mids, nexts, two_send, two_recv, phase, 1, by)

    def three(phase, by):
        return tree(lates, lasts, three_send, three_recv, phase, 2, by)

    def split(value):
        high = value.astype(jnp.bfloat16).astype(jnp.float32)
        rest = value - high
        middle = rest.astype(jnp.bfloat16).astype(jnp.float32)
        return jnp.where(stat_lane < H, high, jnp.where(stat_lane < 2 * H, middle, rest - middle))

    def attend(phase, b):
        width = WS[phase]
        q_ref, part_ref = q_refs[phase], parts[phase]
        slots, stats, places, tags = [], [], [], []
        for n in range(BATCH):
            place = (((b >> 1) + 1) & 3, (b & 1) * 2 + n // SIDE, n % SIDE)
            at = dict(zip(ORDERS[phase], place))
            told = code_smem[(at["y"] << 4) + (at["x"] << 2) + at["z"], 0, 0]
            code = jnp.maximum(told, 0)
            slots.append((code & 1, (code >> 1) & 15, (code >> 5) & 15))
            tags.append(jnp.where(told < 0, -1.0, jnp.where((code & 1) > 0, 1.0, 0.0)))
            places.append(place)
            stats.append(jnp.zeros((QT, LANE), jnp.float32))
        items = [(n, g) for n in range(BATCH) for g in range(width // GW)]
        scores, weights = {}, {}

        def score(n, g):
            which, first, second = slots[n]
            near_cols = slice(g * GW, (g + 1) * GW)
            cols = slice(STARTS[phase] + g * GW, STARTS[phase] + (g + 1) * GW)
            q = jnp.where(
                which > 0, q_ref[(*places[n], slice(QT, 2 * QT), near_cols)], q_ref[(*places[n], slice(0, QT), near_cols)]
            )
            lhs = jnp.concatenate([q * jnp.bfloat16(0.125)] * GH, axis=0) * diag
            k = jnp.concatenate([k_ref[first, :, cols], k_ref[second, :, cols]], axis=0)
            scores[n, g] = lax.dot_general(lhs, k, (((1,), (1,)), ((), ())), preferred_element_type=jnp.float32)

        def weigh(n, g):
            which, first, second = slots[n]
            values = scores.pop((n, g))
            peak = jnp.max(values, axis=1, keepdims=True)
            shaped = jnp.exp(values - peak)
            total = jnp.sum(shaped, axis=1, keepdims=True)
            lse = peak + jnp.log(total * jnp.where(first == second, 0.5, 1.0))
            for h in range(GH):
                head = STARTS[phase] // HD + g * GH + h
                stats[n] = jnp.where(stat_lane % H == head, lse[h * QT : (h + 1) * QT], stats[n])
            weights[n, g] = (shaped.astype(jnp.bfloat16), 1.0 / total)

        def apply(n, g):
            which, first, second = slots[n]
            cols = slice(STARTS[phase] + g * GW, STARTS[phase] + (g + 1) * GW)
            shaped, inverse = weights.pop((n, g))
            v = jnp.concatenate([v_ref[first, :, cols], v_ref[second, :, cols]], axis=0)
            full = jnp.dot(shaped, v, preferred_element_type=jnp.float32)
            for t in range(GW // LANE):
                lanes = slice(t * LANE, (t + 1) * LANE)
                a, b = (slice((2 * t + e) * QT, (2 * t + e + 1) * QT) for e in (0, 1))
                part = jnp.where(near, full[a, lanes] * inverse[a], full[b, lanes] * inverse[b])
                start = g * GW + t * LANE
                part_ref[(*places[n], slice(None), slice(start, start + LANE))] = part.astype(jnp.bfloat16)

        for at in range(len(items) + 4):
            if at < len(items):
                score(*items[at])
            if 2 <= at < len(items) + 2:
                weigh(*items[at - 2])
            if 4 <= at:
                apply(*items[at - 4])
        for n in range(BATCH):
            pieces = jnp.where(stat_lane < 3 * H, split(stats[n]), tags[n])
            part_ref[(*places[n], slice(None), slice(width, width + LANE))] = pieces.astype(jnp.bfloat16)
    fold_row = lax.broadcasted_iota(jnp.int32, (LANE, 2 * LANE), 0)
    fold_lane = lax.broadcasted_iota(jnp.int32, (LANE, 2 * LANE), 1)
    fold = ((fold_lane < LANE) & (fold_row < 3 * H) & (fold_row % H == fold_lane % H)) | (
        (fold_lane >= LANE) & (fold_row == 3 * H)
    )
    fold = fold.astype(jnp.float32).astype(jnp.bfloat16)
    spread_row = lax.broadcasted_iota(jnp.int32, (LANE, GW), 0)
    spread_head = lax.broadcasted_iota(jnp.int32, (LANE, GW), 1) // HD

    def spread(phase, g):
        head = STARTS[phase] // HD + g * GH + spread_head
        chosen = (spread_row < 2 * H) & (spread_row % H == head)
        return chosen.astype(jnp.float32).astype(jnp.bfloat16)

    def merge_first(phase):
        width = WS[phase]
        part_ref, near_ref, mid_ref = parts[phase], nears[phase], mids[phase]

        for by in range(1, SIDE):
            one(phase, by).wait_send()
            one(phase, by).wait_recv()
        count = SIDE * SIDE
        for d in range(SIDE):
            stat = near_ref[d - 1, :, :, :, width:] if d else part_ref[0, :, :, :, width:]
            seen_ref[d] = jnp.dot(stat.reshape(count * QT, LANE), fold, preferred_element_type=jnp.float32)

        def weigh(j, carry):
            rows = pl.ds(pl.multiple_of(j * QT, QT), QT)
            lses = [seen_ref[d, rows, :LANE] for d in range(SIDE)]
            tags = [seen_ref[d, rows, LANE:] for d in range(SIDE)]
            tops = []
            for n in range(2):
                top = jnp.full((QT, LANE), DEAD, jnp.float32)
                for lse, tag in zip(lses, tags):
                    top = jnp.maximum(top, jnp.where(tag == n, lse, DEAD))
                tops.append(top)
            terms = [
                jnp.exp(jnp.minimum(lse - jnp.where(tag == 1.0, tops[1], tops[0]), 0.0)) for lse, tag in zip(lses, tags)
            ]
            inverses = []
            for n in range(2):
                kept = [jnp.where(tag == n, term, 0.0) for term, tag in zip(terms, tags)]
                total = kept[0] + kept[1] + kept[2] + kept[3]
                inverses.append(1.0 / jnp.maximum(total, 1e-30))
                lse = tops[n] + jnp.log(jnp.maximum(total, 1e-30))
                mid_ref[j >> 2, j & 3, n, :, width:] = jnp.where(
                    stat_lane < 3 * H, split(lse), 0.0
                ).astype(jnp.bfloat16)
            for d in range(SIDE):
                share = jnp.where(tags[d] < 0.0, 0.0, terms[d] * jnp.where(tags[d] == 1.0, inverses[1], inverses[0]))
                high = share.astype(jnp.bfloat16).astype(jnp.float32)
                pieces = jnp.where(stat_lane < H, high, jnp.where(stat_lane < 2 * H, share - high, 0.0))
                factor_ref[d, rows, :] = pieces.astype(jnp.bfloat16)
            return carry

        lax.fori_loop(0, count, weigh, 0, unroll=2)
        for g in range(width // GW):
            cols = slice(g * GW, (g + 1) * GW)
            wide_ref[...] = jnp.dot(
                factor_ref[...].reshape(SIDE * count * QT, LANE), spread(phase, g), preferred_element_type=jnp.float32
            ).reshape(SIDE, count * QT, GW)

            def add(j, carry):
                rows = pl.ds(pl.multiple_of(j * QT, QT), QT)
                second, third = j >> 2, j & 3
                blocks = [part_ref[0, second, third, :, cols]]
                blocks += [near_ref[d - 1, second, third, :, cols] for d in range(1, SIDE)]
                totals = [jnp.zeros((QT, GW), jnp.float32)] * 2
                for d in range(SIDE):
                    term = blocks[d].astype(jnp.float32) * wide_ref[d, rows, :]
                    tag = seen_ref[d, rows, LANE:]
                    tag = jnp.concatenate([tag, tag], axis=1)
                    totals = [total + jnp.where(tag == n, term, 0.0) for n, total in enumerate(totals)]
                for n in range(2):
                    mid_ref[second, third, n, :, cols] = totals[n].astype(jnp.bfloat16)
                return carry

            lax.fori_loop(0, count, add, 0, unroll=4)
        for by in range(1, SIDE):
            two(phase, by).start()

    def merge(phase, count, sources, stat_out, data_out):
        width = WS[phase]
        rows = count * QT
        lses = [
            jnp.dot(
                source(slice(width, width + LANE)).reshape(rows, LANE), fold[:, :LANE], preferred_element_type=jnp.float32
            )
            for source in sources
        ]
        top = jnp.maximum(jnp.maximum(lses[0], lses[1]), jnp.maximum(lses[2], lses[3]))
        terms = [jnp.exp(lse - top) for lse in lses]
        total = terms[0] + terms[1] + terms[2] + terms[3]
        inverse = 1.0 / total
        lane = lax.broadcasted_iota(jnp.int32, (rows, LANE), 1)
        for d in range(SIDE):
            share = terms[d] * inverse
            high = share.astype(jnp.bfloat16).astype(jnp.float32)
            pieces = jnp.where(lane < H, high, jnp.where(lane < 2 * H, share - high, 0.0))
            factor_ref[d, :rows, :] = pieces.astype(jnp.bfloat16)
        if stat_out is not None:
            value = top + jnp.log(total)
            high = value.astype(jnp.bfloat16).astype(jnp.float32)
            rest = value - high
            middle = rest.astype(jnp.bfloat16).astype(jnp.float32)
            pieces = jnp.where(lane < H, high, jnp.where(lane < 2 * H, middle, jnp.where(lane < 3 * H, rest - middle, 0.0)))
            stat_out(pieces.astype(jnp.bfloat16))
        for g in range(width // GW):
            cols = slice(g * GW, (g + 1) * GW)
            result = jnp.zeros((rows, GW), jnp.float32)
            for d in range(SIDE):
                wide = jnp.dot(factor_ref[d, :rows, :], spread(phase, g), preferred_element_type=jnp.float32)
                result = result + wide * sources[d](cols).reshape(rows, GW).astype(jnp.float32)
            data_out(cols, result.astype(jnp.bfloat16))

    def merge_second(phase):
        for by in range(1, SIDE):
            two(phase, by).wait_send()
            two(phase, by).wait_recv()
        width, count = WS[phase], 2 * SIDE
        mid_ref, next_ref, late_ref = mids[phase], nexts[phase], lates[phase]

        def source(d):
            if d:
                return lambda cols: next_ref[d - 1, :, :, :, cols].reshape(count, QT, cols.stop - cols.start)
            return lambda cols: mid_ref[0, :, :, :, cols].reshape(count, QT, cols.stop - cols.start)

        def stat_out(value):
            late_ref[:, :, :, width:] = value.reshape(SIDE, 2, QT, LANE)

        def data_out(cols, value):
            late_ref[:, :, :, cols] = value.reshape(SIDE, 2, QT, GW)

        merge(phase, count, [source(d) for d in range(SIDE)], stat_out, data_out)
        for by in range(1, SIDE):
            three(phase, by).start()

    def merge_third(phase):
        for by in range(1, SIDE):
            three(phase, by).wait_send()
            three(phase, by).wait_recv()
        late_ref, last_ref = lates[phase], lasts[phase]

        def source(d):
            return (lambda cols: last_ref[d - 1, :, :, cols]) if d else (lambda cols: late_ref[0, :, :, cols])

        def data_out(cols, value):
            rows = slice(STARTS[phase] + cols.start, STARTS[phase] + cols.stop)
            sum_ref[...] += jnp.dot(value, w_ref[rows, :], preferred_element_type=jnp.float32)

        merge(phase, 2, [source(d) for d in range(SIDE)], None, data_out)

    def run(phase, beside):
        def send(by):
            one(phase, by).start()

        beside = {at: list(acts) for at, acts in beside.items()}
        for by in range(1, SIDE):
            beside.setdefault(2 * by - 1, []).insert(0, (send, by))

        def body(b, carry):
            attend(phase, b)
            for at, acts in beside.items():

                @pl.when(b == at)
                def _():
                    for act, *args in acts:
                        act(*args)

            return carry

        lax.fori_loop(0, OWNERS // BATCH, body, 0)

    def ring_beside(phase):
        return {
            0: [(ring_end, phase, 0), (ring_start, phase, 1)],
            1: [(ring_forward, phase, 1)],
            2: [(ring_end, phase, 1), (ring_start, phase, 2)],
            4: [(ring_forward, phase, 2)],
        }

    run(0, ring_beside(1) | {6: [(ring_start, 2, 0)]})
    ring_end(1, 2)
    ring_forward(2, 0)
    run(1, ring_beside(2))
    ring_end(2, 2)
    merge_first(0)
    run(2, {})
    merge_first(1)
    merge_second(0)
    merge_first(2)
    merge_second(1)
    sum_ref[...] = jnp.zeros(sum_ref.shape, jnp.float32)
    w_home.wait()
    w_give.wait_send()
    w_take.wait_recv()
    merge_third(0)
    merge_second(2)
    merge_third(1)
    for phase in range(3):
        ring_sent(phase)
    for stage in range(3):
        for by in range(1, SIDE):
            list_copy(stage, by).wait_send()
    merge_third(2)
    out_ref[...] = sum_ref[...].astype(jnp.bfloat16)


def on_device(queries, keys, values, counts, passage_ids, out_weight):
    list_len = passage_ids.shape[1]
    listed = jnp.arange(list_len)[None, :] < counts[:, None]
    ids = jnp.where(listed, passage_ids, -1).astype(jnp.int32)
    ids = jnp.pad(ids, ((0, 0), (0, LANE // 2 - list_len)), constant_values=-1).reshape(1, LANE)
    bf16 = [pltpu.VMEM((SIDE, SIDE, SIDE, 2 * QT, width), jnp.bfloat16) for width in WS]
    for lead in (
        (SIDE, SIDE, SIDE),
        (SIDE - 1, SIDE, SIDE),
        (SIDE, SIDE, 2),
        (SIDE - 1, SIDE, 2),
        (SIDE, 2),
        (SIDE - 1, 2),
    ):
        bf16 += [pltpu.VMEM((*lead, QT, width + LANE), jnp.bfloat16) for width in WS]
    plane = SIDE * SIDE * QT
    return pl.pallas_call(
        torus_kernel,
        out_shape=jax.ShapeDtypeStruct((2 * QT, D), jnp.bfloat16),
        in_specs=[pl.BlockSpec(memory_space=pltpu.VMEM)] * 2 + [pl.BlockSpec(memory_space=pl.ANY)] * 3,
        out_specs=pl.BlockSpec(memory_space=pltpu.VMEM),
        scratch_shapes=bf16
        + [
            pltpu.VMEM(keys.shape, jnp.bfloat16),
            pltpu.VMEM(values.shape, jnp.bfloat16),
            pltpu.VMEM((D, D), jnp.bfloat16),
            pltpu.VMEM((SIDE, SIDE, SIDE, 1, LANE), jnp.int32),
            pltpu.VMEM((OWNERS, 1, LANE), jnp.int32),
            pltpu.SMEM((OWNERS, 1, LANE), jnp.int32),
            pltpu.VMEM((SIDE, plane, 2 * LANE), jnp.float32),
            pltpu.VMEM((SIDE, plane, LANE), jnp.bfloat16),
            pltpu.VMEM((SIDE, plane, GW), jnp.float32),
            pltpu.VMEM((2 * QT, D), jnp.float32),
            pltpu.SemaphoreType.DMA((2,)),
            pltpu.SemaphoreType.DMA((5,)),
            pltpu.SemaphoreType.DMA((3, SIDE)),
            pltpu.SemaphoreType.DMA((3, SIDE)),
            pltpu.SemaphoreType.DMA((2,)),
            pltpu.SemaphoreType.DMA((3, 3, 3, 4)),
            pltpu.SemaphoreType.DMA((3, 3, 3, 4)),
        ]
        + [pltpu.SemaphoreType.DMA((3, SIDE))] * 6,
        compiler_params=pltpu.CompilerParams(
            vmem_limit_bytes=60 * 2**20, collective_id=0, has_side_effects=True
        ),
        cost_estimate=pl.CostEstimate(flops=40 * 10**9, bytes_accessed=20 * 2**20, transcendentals=4 * 10**6),
        name="torus",
    )(ids, queries, keys, values, out_weight)


def solution(mesh):
    placed = (
        P(("grp", "dev"), None),
        P(("grp", "dev"), None, None),
        P(("grp", "dev"), None, None),
        P(("grp", "dev")),
        P(("grp", "dev"), None),
        P("grp", None),
    )
    return jax.shard_map(
        on_device, mesh=mesh, in_specs=placed, out_specs=P(("grp", "dev"), None), check_vma=False
    )
```

time: 142 us -> 151 us (1.063); the launches traced: 140 us -> 150 us
  Pallas kernels: 137 us -> 148 us
    pallas_call x1, Pallas kernels: 137 us -> 148 us  [on_device(): pl.pallas_call(torus_kernel, out_shape=jax.ShapeDtypeStruct((2 * QT, D),...]
where the time goes in v2:
time: 151 us; the launch traced here: 150 us
  Pallas kernels  148 us (98%)
  local copies, waits for them, and re-layouts  2.17 us (1%)
    pallas_call x1, Pallas kernels, on_device(): pl.pallas_call(torus_kernel, out_shape=jax.ShapeDtypeStruct((2 * QT, D),...  148 us

profile of v2, /device:TPU:0, one launch (start us, length us, event | category | flops | bytes accessed | tf_op | source)
XLA Modules:
  0.0 150.4 jit_solution(7395193027361721046)
XLA Ops:
  0.0 0.8 compare_select_fusion
  0.8 0.6 reshape.4.ids_ref
  1.4 147.5 %torus.1 = bf16[32,2048]{1,0:T(8,128)(2,1)} custom-call(s32[1,128]{1,0:T(1,128)} %reshape.4.ids_ref, bf16[32,2048]{1,0:T(8,128)(2,1)} %mine_ref.1, bf16[16,64,2048]{2,1,0:T(8,128)(2,1)} %k_hbm.1, bf16[16,64,2048]{2,1,0:T(8,128)(2,1)} %v_hbm.1, bf16[1024,2048]{1,0:T(8,128)(2,1)} %w_hbm.1), custom_call_target="tpu_custom_call" | custom-call | flops 40000000000 | bytes 20971520 | tf_op jit(solution)/shard_map/torus/pallas_call | solution.py:533
  148.9 1.6 %copy.8 = bf16[32,2048]{1,0:T(8,128)(2,1)} copy(bf16[32,2048]{1,0:T(8,128)(2,1)} %torus.1) | data formatting | bytes 262144
  (1 shorter events, 0.0 us)

commit v3 on v2

v3 whole, which is shorter than its diff:
```python
import jax
import jax.numpy as jnp
from jax import lax
from jax.experimental import pallas as pl
from jax.experimental.pallas import tpu as pltpu
from jax.sharding import PartitionSpec as P

D = 2048
H = 32
HD = 64
QT = 16
PT = 64
GW = 256
GH = GW // HD
GROUPS = D // GW
LANE = 128
SIDE = 4
OWNERS = SIDE * SIDE * SIDE
PHASES = ((0, 1, 2), (3, 4, 5), (6, 7))
BATCH = 8
DEAD = -1e30
ORDERS = (("x", "y", "z"), ("y", "z", "x"), ("z", "x", "y"))
MESH = pl.DeviceIdType.MESH


def torus_kernel(
    ids_ref, mine_ref, k_hbm, v_hbm, w_hbm, out_ref,
    q_ref, part_ref, near_ref, mid_ref, next_ref, late_ref, last_ref,
    part_stat, near_stat, mid_stat, next_stat, late_stat, last_stat,
    k_ref, v_ref, w_ref, list_ref, code_ref, code_smem, spread_one, spread_two, spread_three, attended_ref, sum_ref,
    load_sem, home_sem, list_send, list_recv, w_sem, ring_send, ring_recv, tree_send, tree_recv,
):
    me = lax.axis_index("dev")
    grp = lax.axis_index("grp")
    own = {"y": me >> 4, "x": (me >> 2) & 3, "z": me & 3}
    stride = {"y": SIDE * SIDE, "x": SIDE, "z": 1}
    line = {
        axis: {by: (grp, me + ((((own[axis] + by) & 3) - own[axis]) * stride[axis])) for by in range(1, SIDE)}
        for axis in own
    }
    loads = [
        pltpu.make_async_copy(k_hbm, k_ref, load_sem.at[0]),
        pltpu.make_async_copy(v_hbm, v_ref, load_sem.at[1]),
    ]
    for load in loads:
        load.start()
    barrier = pltpu.get_barrier_semaphore()
    for axis in line:
        for by in line[axis]:
            pl.semaphore_signal(barrier, inc=1, device_id=line[axis][by], device_id_type=MESH)
    pl.semaphore_signal(barrier, inc=1, device_id=(1 - grp, me), device_id_type=MESH)
    homes = [
        pltpu.make_async_copy(mine_ref.at[:, pl.ds(g * GW, GW)], q_ref.at[g, 0, 0, 0], home_sem.at[g])
        for g in range(GROUPS)
    ]
    for home in homes:
        home.start()
    list_ref[0, 0, 0] = ids_ref[...]
    pl.semaphore_wait(barrier, 10)

    whole, lower, upper = (0, 2 * QT), (0, QT), (QT, QT)
    both = ((0, 1, 3, lower), (1, 3, 1, upper))

    def order_of(g):
        return ORDERS[g % 3]

    def ring_block(g, stage, at, rows):
        spot = [pl.ds(0, SIDE) if n < stage else at if n == stage else 0 for n in range(3)]
        return q_ref.at[g, spot[0], spot[1], spot[2], pl.ds(*rows), :]

    def ring_own(g, stage, kind, by, at):
        source = ring_block(g, stage, 0, whole) if stage else mine_ref.at[:, pl.ds(g * GW, GW)]
        return pltpu.make_async_remote_copy(
            src_ref=source,
            dst_ref=ring_block(g, stage, at, whole),
            send_sem=ring_send.at[g, stage, kind],
            recv_sem=ring_recv.at[g, stage, kind],
            device_id=line[order_of(g)[stage]][by],
            device_id_type=MESH,
        )

    def ring_pass(g, stage, kind, by, at, rows):
        return pltpu.make_async_remote_copy(
            src_ref=ring_block(g, stage, at, rows),
            dst_ref=ring_block(g, stage, 2, rows),
            send_sem=ring_send.at[g, stage, 2 + kind],
            recv_sem=ring_recv.at[g, stage, 2 + kind],
            device_id=line[order_of(g)[stage]][by],
            device_id_type=MESH,
        )

    def ring_start(phase, stage):
        for g in PHASES[phase]:
            for kind, by, at, rows in both:
                ring_own(g, stage, kind, by, at).start()

    def ring_forward(phase, stage):
        for kind, by, at, rows in both:
            for g in PHASES[phase]:
                ring_own(g, stage, kind, by, at).wait_recv()
                ring_pass(g, stage, kind, by, at, rows).start()

    def ring_end(phase, stage):
        for g in PHASES[phase]:
            for kind, by, at, rows in both:
                ring_pass(g, stage, kind, by, at, rows).wait_recv()

    def ring_sent():
        for g in range(GROUPS):
            for stage in range(3):
                for kind, by, at, rows in both:
                    ring_own(g, stage, kind, by, at).wait_send()
                    ring_pass(g, stage, kind, by, at, rows).wait_send()

    def list_copy(stage, by):
        order = ("x", "y", "z")
        spot = {axis: 0 for axis in order}
        for axis in order[:stage]:
            spot[axis] = pl.ds(0, SIDE)
        source = list_ref.at[spot["y"], spot["x"], spot["z"]]
        spot[order[stage]] = SIDE - by
        return pltpu.make_async_remote_copy(
            src_ref=source,
            dst_ref=list_ref.at[spot["y"], spot["x"], spot["z"]],
            send_sem=list_send.at[stage, by],
            recv_sem=list_recv.at[stage, by],
            device_id=line[order[stage]][by],
            device_id_type=MESH,
        )

    def list_start(stage):
        for by in range(1, SIDE):
            list_copy(stage, by).start()

    def list_end(stage):
        for by in range(1, SIDE):
            list_copy(stage, by).wait_recv()

    w_rows = D // 2
    w_home = pltpu.make_async_copy(w_hbm, w_ref.at[pl.ds(grp * w_rows, w_rows)], load_sem.at[2])
    w_give = pltpu.make_async_remote_copy(
        src_ref=w_hbm,
        dst_ref=w_ref.at[pl.ds(grp * w_rows, w_rows)],
        send_sem=w_sem.at[0],
        recv_sem=w_sem.at[1],
        device_id=(1 - grp, me),
        device_id_type=MESH,
    )
    w_take = pltpu.make_async_remote_copy(
        src_ref=w_hbm,
        dst_ref=w_ref.at[pl.ds((1 - grp) * w_rows, w_rows)],
        send_sem=w_sem.at[0],
        recv_sem=w_sem.at[1],
        device_id=(1 - grp, me),
        device_id_type=MESH,
    )

    list_start(0)
    ring_start(0, 0)
    part_stat[...] = jnp.zeros(part_stat.shape, jnp.float32)
    spread_row = lax.broadcasted_iota(jnp.int32, (LANE, GW), 0)
    spread_head = lax.broadcasted_iota(jnp.int32, (LANE, GW), 1) >> 6
    in_half = spread_row & 63

    def as_matrix(chosen):
        return chosen.astype(jnp.float32).astype(jnp.bfloat16)

    for n in range(SIDE * SIDE):
        spread_one[n] = as_matrix(in_half == n * GH + spread_head)
    for n in range(2 * SIDE):
        chosen = (in_half < 32) & ((in_half & 15) == (n >> 1) * GH + spread_head)
        spread_two[n] = as_matrix(chosen & ((spread_row >> 6) == (n & 1)))
    for n in range(2):
        chosen = (in_half < 8) & ((in_half & 3) == spread_head)
        spread_three[n] = as_matrix(chosen & ((spread_row >> 6) == n))
    for home in homes:
        home.wait()
    list_end(0)
    list_start(1)
    ring_forward(0, 0)
    list_end(1)
    list_start(2)
    ring_end(0, 0)
    ring_start(0, 1)
    ring_forward(0, 1)
    ring_end(0, 1)
    ring_start(0, 2)
    list_end(2)
    ids = list_ref[...].reshape(OWNERS, LANE)
    key = lax.broadcasted_iota(jnp.int32, (OWNERS, LANE), 1) * 16 + (ids & 15)
    here = (ids >> 4) == me
    first = jnp.min(jnp.where(here, key, 1 << 20), axis=1, keepdims=True)
    last = jnp.max(jnp.where(here, key, -1), axis=1, keepdims=True)
    code = jnp.where(last < 0, -1, (first >> 10) + ((first & 15) << 1) + ((last & 15) << 5))
    code_ref[...] = jnp.broadcast_to(code, (OWNERS, LANE)).reshape(OWNERS, 1, LANE)
    code_move = pltpu.make_async_copy(code_ref, code_smem, load_sem.at[3])
    code_move.start()
    ring_forward(0, 2)
    ring_start(1, 0)
    w_home.start()
    w_give.start()
    for load in loads:
        load.wait()
    code_move.wait()
    ring_end(0, 2)
    ring_forward(1, 0)

    row_head = lax.broadcasted_iota(jnp.int32, (GH * QT, GW), 0) // QT
    lane_head = lax.broadcasted_iota(jnp.int32, (GH * QT, GW), 1) // HD
    diag = (row_head == lane_head).astype(jnp.float32).astype(jnp.bfloat16)
    stat_lane = lax.broadcasted_iota(jnp.int32, (QT, LANE), 1)
    near = stat_lane < HD

    def tree(sources, targets, g, stage, by):
        return [
            pltpu.make_async_remote_copy(
                src_ref=source,
                dst_ref=target,
                send_sem=tree_send.at[stage, g, by, n],
                recv_sem=tree_recv.at[stage, g, by, n],
                device_id=line[order_of(g)[stage]][by],
                device_id_type=MESH,
            )
            for n, (source, target) in enumerate(zip(sources, targets))
        ]

    def one(g, by):
        return tree(
            (part_ref.at[g, by], part_stat.at[g, by]), (near_ref.at[g, by - 1], near_stat.at[g, by - 1]), g, 0, by
        )

    def two(g, by):
        return tree((mid_ref.at[g, by], mid_stat.at[g]), (next_ref.at[g, by - 1], next_stat.at[g, by - 1]), g, 1, by)

    def three(g, by):
        return tree((late_ref.at[g, by], late_stat.at[g]), (last_ref.at[g, by - 1], last_stat.at[g, by - 1]), g, 2, by)

    def tree_start(stage, g):
        for by in range(1, SIDE):
            for copy in stage(g, by):
                copy.start()

    def tree_wait(stage, g):
        for by in range(1, SIDE):
            for copy in stage(g, by):
                copy.wait_send()
                copy.wait_recv()

    stride = {"y": SIDE * SIDE, "x": SIDE, "z": 1}

    def attend(phase, b):
        delta, part_half = ((b >> 1) + 1) & 3, b & 1
        items = [(n, g) for n in range(BATCH) for g in PHASES[phase]]
        slots, tags, scores, weights = {}, {}, {}, {}
        lane = stat_lane - part_half * (BATCH * GH)
        stats = {g: part_stat[g, delta] for g in PHASES[phase]}

        def place(n):
            return delta, part_half * 2 + n // SIDE, n % SIDE

        for n, g in items:
            told = code_smem[sum(at * stride[axis] for axis, at in zip(order_of(g), place(n))), 0, 0]
            code = jnp.maximum(told, 0)
            slots[n, g] = (code & 1, (code >> 1) & 15, (code >> 5) & 15)
            tags[n, g] = jnp.where(told < 0, -1.0, jnp.where((code & 1) > 0, 1.0, 0.0))

        def score(n, g):
            which, first, second = slots[n, g]
            cols = slice(g * GW, (g + 1) * GW)
            q = jnp.where(which > 0, q_ref[(g, *place(n), slice(QT, 2 * QT))], q_ref[(g, *place(n), slice(0, QT))])
            lhs = jnp.concatenate([q * jnp.bfloat16(0.125)] * GH, axis=0) * diag
            k = jnp.concatenate([k_ref[first, :, cols], k_ref[second, :, cols]], axis=0)
            scores[n, g] = lax.dot_general(lhs, k, (((1,), (1,)), ((), ())), preferred_element_type=jnp.float32)

        def weigh(n, g):
            which, first, second = slots[n, g]
            values = scores.pop((n, g))
            peak = jnp.max(values, axis=1, keepdims=True)
            shaped = jnp.exp(values - peak)
            total = jnp.sum(shaped, axis=1, keepdims=True)
            lse = peak + jnp.log(total * jnp.where(first == second, 0.5, 1.0))
            for h in range(GH):
                stats[g] = jnp.where(lane == n * GH + h, lse[h * QT : (h + 1) * QT], stats[g])
            stats[g] = jnp.where(((lane - LANE // 2) >> 2) == n, tags[n, g], stats[g])
            weights[n, g] = (shaped.astype(jnp.bfloat16), 1.0 / total)

        def apply(n, g):
            which, first, second = slots[n, g]
            cols = slice(g * GW, (g + 1) * GW)
            shaped, inverse = weights.pop((n, g))
            v = jnp.concatenate([v_ref[first, :, cols], v_ref[second, :, cols]], axis=0)
            full = jnp.dot(shaped, v, preferred_element_type=jnp.float32)
            for t in range(GW // LANE):
                lanes = slice(t * LANE, (t + 1) * LANE)
                a, c = (slice((2 * t + e) * QT, (2 * t + e + 1) * QT) for e in (0, 1))
                part = jnp.where(near, full[a, lanes] * inverse[a], full[c, lanes] * inverse[c])
                part_ref[(g, *place(n), slice(None), lanes)] = part.astype(jnp.bfloat16)

        for at in range(len(items) + 4):
            if at < len(items):
                score(*items[at])
            if 2 <= at < len(items) + 2:
                weigh(*items[at - 2])
            if 4 <= at:
                apply(*items[at - 4])
        for g in PHASES[phase]:
            part_stat[g, delta] = stats[g]

    def rounded(value):
        return value.astype(jnp.bfloat16).astype(jnp.float32)

    def blend(factors, matrix, blocks):
        wide = jnp.dot(factors, matrix, preferred_element_type=jnp.float32)
        sums = []
        for at in range(0, factors.shape[0] // QT, SIDE):
            total = blocks[0] * wide[at * QT : (at + 1) * QT]
            for d in range(1, SIDE):
                total = total + blocks[d] * wide[(at + d) * QT : (at + d + 1) * QT]
            sums.append(total)
        return sums

    def merge_one(g):
        tree_wait(one, g)
        packed = [part_stat[g, 0]] + [near_stat[g, d - 1] for d in range(1, SIDE)]
        tags = [pltpu.roll(stat, LANE // 2, 1) for stat in packed]
        tops = []
        for n in range(2):
            kept = [jnp.where(tag == n, stat, DEAD) for stat, tag in zip(packed, tags)]
            tops.append(jnp.maximum(jnp.maximum(kept[0], kept[1]), jnp.maximum(kept[2], kept[3])))
        terms = [
            jnp.exp(jnp.minimum(stat - jnp.where(tag == 1.0, tops[1], tops[0]), 0.0)) for stat, tag in zip(packed, tags)
        ]
        factors, results = [], []
        for n in range(2):
            kept = [jnp.where(tag == n, term, 0.0) for term, tag in zip(terms, tags)]
            total = jnp.maximum(kept[0] + kept[1] + kept[2] + kept[3], 1e-30)
            results.append(tops[n] + jnp.log(total))
            for term in kept:
                share = term / total
                high = rounded(share)
                factors.append(jnp.where(stat_lane < LANE // 2, high, pltpu.roll(share - high, LANE // 2, 1)))
        mid_stat[g] = jnp.where(stat_lane < LANE // 2, results[0], pltpu.roll(results[1], LANE // 2, 1))
        factors = jnp.concatenate(factors, axis=0).astype(jnp.bfloat16)

        def body(j, carry):
            second, third = j >> 2, j & 3
            blocks = [part_ref[g, 0, second, third]] + [near_ref[g, d - 1, second, third] for d in range(1, SIDE)]
            sums = blend(factors, spread_one[j], [block.astype(jnp.float32) for block in blocks])
            for n in range(2):
                mid_ref[g, second, third, n] = sums[n].astype(jnp.bfloat16)
            return carry

        lax.fori_loop(0, SIDE * SIDE, body, 0, unroll=4)
        tree_start(two, g)

    def shares_of(packed, span):
        top = jnp.maximum(jnp.maximum(packed[0], packed[1]), jnp.maximum(packed[2], packed[3]))
        terms = [jnp.exp(stat - top) for stat in packed]
        total = terms[0] + terms[1] + terms[2] + terms[3]
        factors = []
        for term in terms:
            share = term / total
            high = rounded(share)
            low = pltpu.roll(share - high, span, 1)
            in_lane = stat_lane & 63
            factors.append(jnp.where(in_lane < span, high, jnp.where(in_lane < 2 * span, low, 0.0)))
        return top + jnp.log(total), jnp.concatenate(factors, axis=0).astype(jnp.bfloat16)

    def merge_two(g):
        tree_wait(two, g)
        packed = [mid_stat[g]] + [pltpu.roll(next_stat[g, d - 1], LANE - 16 * d, 1) for d in range(1, SIDE)]
        late_stat[g], factors = shares_of(packed, 16)
        for third in range(SIDE):
            for n in range(2):
                blocks = [mid_ref[g, 0, third, n]] + [next_ref[g, d - 1, third, n] for d in range(1, SIDE)]
                sums = blend(factors, spread_two[third * 2 + n], [block.astype(jnp.float32) for block in blocks])
                late_ref[g, third, n] = sums[0].astype(jnp.bfloat16)
        tree_start(three, g)

    def merge_three(g):
        tree_wait(three, g)
        packed = [late_stat[g]] + [pltpu.roll(last_stat[g, d - 1], LANE - 4 * d, 1) for d in range(1, SIDE)]
        value, factors = shares_of(packed, 4)
        for n in range(2):
            blocks = [late_ref[g, 0, n]] + [last_ref[g, d - 1, n] for d in range(1, SIDE)]
            sums = blend(factors, spread_three[n], [block.astype(jnp.float32) for block in blocks])
            attended_ref[n * QT : (n + 1) * QT, g * GW : (g + 1) * GW] = sums[0].astype(jnp.bfloat16)

    def project(phase):
        rows = slice(PHASES[phase][0] * GW, (PHASES[phase][-1] + 1) * GW)
        product = jnp.dot(attended_ref[:, rows], w_ref[rows, :], preferred_element_type=jnp.float32)
        if phase == 0:
            sum_ref[...] = product
        elif phase == 1:
            sum_ref[...] += product
        else:
            out_ref[...] = (sum_ref[...] + product).astype(jnp.bfloat16)

    def run(phase, beside):
        def send(by):
            for g in PHASES[phase]:
                for copy in one(g, by):
                    copy.start()

        beside = {at: list(acts) for at, acts in beside.items()}
        for by in range(1, SIDE):
            beside.setdefault(2 * by - 1, []).insert(0, (send, by))

        def body(b, carry):
            attend(phase, b)
            for at, acts in beside.items():

                @pl.when(b == at)
                def _():
                    for act, *args in acts:
                        act(*args)

            return carry

        lax.fori_loop(0, OWNERS // BATCH, body, 0)

    def ring_beside(phase):
        return {
            0: [(ring_end, phase, 0), (ring_start, phase, 1)],
            1: [(ring_forward, phase, 1)],
            2: [(ring_end, phase, 1), (ring_start, phase, 2)],
            4: [(ring_forward, phase, 2)],
        }

    def each(merge, phase):
        for g in PHASES[phase]:
            merge(g)

    run(0, ring_beside(1) | {6: [(ring_start, 2, 0)]})
    ring_end(1, 2)
    ring_forward(2, 0)
    run(1, ring_beside(2))
    ring_end(2, 2)
    each(merge_one, 0)
    run(2, {})
    each(merge_one, 1)
    each(merge_two, 0)
    each(merge_one, 2)
    each(merge_two, 1)
    each(merge_three, 0)
    w_home.wait()
    w_give.wait_send()
    w_take.wait_recv()
    project(0)
    each(merge_two, 2)
    each(merge_three, 1)
    project(1)
    ring_sent()
    for stage in range(3):
        for by in range(1, SIDE):
            list_copy(stage, by).wait_send()
    each(merge_three, 2)
    project(2)


def on_device(queries, keys, values, counts, passage_ids, out_weight):
    list_len = passage_ids.shape[1]
    listed = jnp.arange(list_len)[None, :] < counts[:, None]
    ids = jnp.where(listed, passage_ids, -1).astype(jnp.int32)
    ids = jnp.pad(ids, ((0, 0), (0, LANE // 2 - list_len)), constant_values=-1).reshape(1, LANE)
    leads = (
        (SIDE, SIDE, SIDE),
        (SIDE - 1, SIDE, SIDE),
        (SIDE, SIDE, 2),
        (SIDE - 1, SIDE, 2),
        (SIDE, 2),
        (SIDE - 1, 2),
    )
    blocks = [pltpu.VMEM((GROUPS, SIDE, SIDE, SIDE, 2 * QT, GW), jnp.bfloat16)]
    blocks += [pltpu.VMEM((GROUPS, *lead, QT, GW), jnp.bfloat16) for lead in leads]
    for lead in ((SIDE,), (SIDE - 1,), (), (SIDE - 1,), (), (SIDE - 1,)):
        blocks.append(pltpu.VMEM((GROUPS, *lead, QT, LANE), jnp.float32))
    return pl.pallas_call(
        torus_kernel,
        out_shape=jax.ShapeDtypeStruct((2 * QT, D), jnp.bfloat16),
        in_specs=[pl.BlockSpec(memory_space=pltpu.VMEM)] * 2 + [pl.BlockSpec(memory_space=pl.ANY)] * 3,
        out_specs=pl.BlockSpec(memory_space=pltpu.VMEM),
        scratch_shapes=blocks
        + [
            pltpu.VMEM(keys.shape, jnp.bfloat16),
            pltpu.VMEM(values.shape, jnp.bfloat16),
            pltpu.VMEM((D, D), jnp.bfloat16),
            pltpu.VMEM((SIDE, SIDE, SIDE, 1, LANE), jnp.int32),
            pltpu.VMEM((OWNERS, 1, LANE), jnp.int32),
            pltpu.SMEM((OWNERS, 1, LANE), jnp.int32),
            pltpu.VMEM((SIDE * SIDE, LANE, GW), jnp.bfloat16),
            pltpu.VMEM((2 * SIDE, LANE, GW), jnp.bfloat16),
            pltpu.VMEM((2, LANE, GW), jnp.bfloat16),
            pltpu.VMEM((2 * QT, D), jnp.bfloat16),
            pltpu.VMEM((2 * QT, D), jnp.float32),
            pltpu.SemaphoreType.DMA((4,)),
            pltpu.SemaphoreType.DMA((GROUPS,)),
            pltpu.SemaphoreType.DMA((3, SIDE)),
            pltpu.SemaphoreType.DMA((3, SIDE)),
            pltpu.SemaphoreType.DMA((2,)),
            pltpu.SemaphoreType.DMA((GROUPS, 3, 4)),
            pltpu.SemaphoreType.DMA((GROUPS, 3, 4)),
            pltpu.SemaphoreType.DMA((3, GROUPS, SIDE, 2)),
            pltpu.SemaphoreType.DMA((3, GROUPS, SIDE, 2)),
        ],
        compiler_params=pltpu.CompilerParams(
            vmem_limit_bytes=60 * 2**20, collective_id=0, has_side_effects=True
        ),
        cost_estimate=pl.CostEstimate(flops=40 * 10**9, bytes_accessed=20 * 2**20, transcendentals=4 * 10**6),
        name="torus",
    )(ids, queries, keys, values, out_weight)


def solution(mesh):
    placed = (
        P(("grp", "dev"), None),
        P(("grp", "dev"), None, None),
        P(("grp", "dev"), None, None),
        P(("grp", "dev")),
        P(("grp", "dev"), None),
        P("grp", None),
    )
    return jax.shard_map(
        on_device, mesh=mesh, in_specs=placed, out_specs=P(("grp", "dev"), None), check_vma=False
    )
```

time: 151 us -> 130 us (0.86)
  Pallas kernels: 148 us -> 127 us
    pallas_call x1, Pallas kernels: 148 us -> 127 us  [on_device(): pl.pallas_call(torus_kernel, out_shape=jax.ShapeDtypeStruct((2 * QT, D),...]
where the time goes in v3:
time: 130 us
  Pallas kernels  127 us (98%)
  local copies, waits for them, and re-layouts  2.17 us (2%)
    pallas_call x1, Pallas kernels, on_device(): pl.pallas_call(torus_kernel, out_shape=jax.ShapeDtypeStruct((2 * QT, D),...  127 us

profile of v3, /device:TPU:0, one launch (start us, length us, event | category | flops | bytes accessed | tf_op | source)
XLA Modules:
  0.0 129.5 jit_solution(18133595337240131673)
XLA Ops:
  0.0 0.8 compare_select_fusion
  0.8 0.6 reshape.4.ids_ref
  1.4 126.6 %torus.1 = bf16[32,2048]{1,0:T(8,128)(2,1)} custom-call(s32[1,128]{1,0:T(1,128)} %reshape.4.ids_ref, bf16[32,2048]{1,0:T(8,128)(2,1)} %mine_ref.1, bf16[16,64,2048]{2,1,0:T(8,128)(2,1)} %k_hbm.1, bf16[16,64,2048]{2,1,0:T(8,128)(2,1)} %v_hbm.1, bf16[1024,2048]{1,0:T(8,128)(2,1)} %w_hbm.1), custom_call_target="tpu_custom_call" | custom-call | flops 40000000000 | bytes 20971520 | tf_op jit(solution)/shard_map/torus/pallas_call | solution.py:478
  127.9 1.6 %copy.8 = bf16[32,2048]{1,0:T(8,128)(2,1)} copy(bf16[32,2048]{1,0:T(8,128)(2,1)} %torus.1) | data formatting | bytes 262144
  (1 shorter events, 0.0 us)

commit v4 on v3

--- a/solution.py
+++ b/solution.py
@@ -24,10 +24,10 @@
 
 
 def torus_kernel(
-    ids_ref, mine_ref, k_hbm, v_hbm, w_hbm, out_ref,
+    counts_ref, ids_ref, mine_ref, k_hbm, v_hbm, w_hbm, out_ref,
     q_ref, part_ref, near_ref, mid_ref, next_ref, late_ref, last_ref,
     part_stat, near_stat, mid_stat, next_stat, late_stat, last_stat,
-    k_ref, v_ref, w_ref, list_ref, code_ref, code_smem, spread_one, spread_two, spread_three, attended_ref, sum_ref,
+    k_ref, v_ref, w_ref, list_ref, code_ref, code_smem, attended_ref, sum_ref,
     load_sem, home_sem, list_send, list_recv, w_sem, ring_send, ring_recv, tree_send, tree_recv,
 ):
     me = lax.axis_index("dev")
@@ -55,11 +55,20 @@
     ]
     for home in homes:
         home.start()
-    list_ref[0, 0, 0] = ids_ref[...]
+    list_len = ids_ref.shape[1]
+    place = lax.broadcasted_iota(jnp.int32, (2, list_len), 1)
+    row = lax.broadcasted_iota(jnp.int32, (2, list_len), 0)
+    live = place < jnp.where(row == 0, counts_ref[0], counts_ref[1])
+    list_ref[0, 0, 0] = jnp.full((2, LANE), -1, jnp.int32)
+    list_ref[0, 0, 0, :, :list_len] = jnp.where(live, ids_ref[...], -1)
     pl.semaphore_wait(barrier, 10)
 
     whole, lower, upper = (0, 2 * QT), (0, QT), (QT, QT)
     both = ((0, 1, 3, lower), (1, 3, 1, upper))
+    straight = both + ((2, 2, 2, whole),)
+
+    def sends(stage):
+        return both if stage == 2 else straight
 
     def order_of(g):
         return ORDERS[g % 3]
@@ -91,7 +100,7 @@
 
     def ring_start(phase, stage):
         for g in PHASES[phase]:
-            for kind, by, at, rows in both:
+            for kind, by, at, rows in sends(stage):
                 ring_own(g, stage, kind, by, at).start()
 
     def ring_forward(phase, stage):
@@ -102,15 +111,19 @@
 
     def ring_end(phase, stage):
         for g in PHASES[phase]:
-            for kind, by, at, rows in both:
-                ring_pass(g, stage, kind, by, at, rows).wait_recv()
+            for kind, by, at, rows in sends(stage):
+                if stage == 2:
+                    ring_pass(g, stage, kind, by, at, rows).wait_recv()
+                else:
+                    ring_own(g, stage, kind, by, at).wait_recv()
 
     def ring_sent():
         for g in range(GROUPS):
             for stage in range(3):
-                for kind, by, at, rows in both:
+                for kind, by, at, rows in sends(stage):
                     ring_own(g, stage, kind, by, at).wait_send()
-                    ring_pass(g, stage, kind, by, at, rows).wait_send()
+                    if stage == 2:
+                        ring_pass(g, stage, kind, by, at, rows).wait_send()
 
     def list_copy(stage, by):
         order = ("x", "y", "z")
@@ -158,39 +171,25 @@
     list_start(0)
     ring_start(0, 0)
     part_stat[...] = jnp.zeros(part_stat.shape, jnp.float32)
-    spread_row = lax.broadcasted_iota(jnp.int32, (LANE, GW), 0)
-    spread_head = lax.broadcasted_iota(jnp.int32, (LANE, GW), 1) >> 6
-    in_half = spread_row & 63
-
-    def as_matrix(chosen):
-        return chosen.astype(jnp.float32).astype(jnp.bfloat16)
-
-    for n in range(SIDE * SIDE):
-        spread_one[n] = as_matrix(in_half == n * GH + spread_head)
-    for n in range(2 * SIDE):
-        chosen = (in_half < 32) & ((in_half & 15) == (n >> 1) * GH + spread_head)
-        spread_two[n] = as_matrix(chosen & ((spread_row >> 6) == (n & 1)))
-    for n in range(2):
-        chosen = (in_half < 8) & ((in_half & 3) == spread_head)
-        spread_three[n] = as_matrix(chosen & ((spread_row >> 6) == n))
     for home in homes:
         home.wait()
     list_end(0)
     list_start(1)
-    ring_forward(0, 0)
+    ring_end(0, 0)
+    ring_start(0, 1)
     list_end(1)
     list_start(2)
-    ring_end(0, 0)
-    ring_start(0, 1)
-    ring_forward(0, 1)
     ring_end(0, 1)
     ring_start(0, 2)
     list_end(2)
-    ids = list_ref[...].reshape(OWNERS, LANE)
-    key = lax.broadcasted_iota(jnp.int32, (OWNERS, LANE), 1) * 16 + (ids & 15)
-    here = (ids >> 4) == me
-    first = jnp.min(jnp.where(here, key, 1 << 20), axis=1, keepdims=True)
-    last = jnp.max(jnp.where(here, key, -1), axis=1, keepdims=True)
+    firsts, lasts = [], []
+    for n in range(2):
+        ids = list_ref[:, :, :, n, :].reshape(OWNERS, LANE)
+        key = n * 1024 + lax.broadcasted_iota(jnp.int32, (OWNERS, LANE), 1) * 16 + (ids & 15)
+        here = (ids >> 4) == me
+        firsts.append(jnp.min(jnp.where(here, key, 1 << 20), axis=1, keepdims=True))
+        lasts.append(jnp.max(jnp.where(here, key, -1), axis=1, keepdims=True))
+    first, last = jnp.minimum(*firsts), jnp.maximum(*lasts)
     code = jnp.where(last < 0, -1, (first >> 10) + ((first & 15) << 1) + ((last & 15) << 5))
     code_ref[...] = jnp.broadcast_to(code, (OWNERS, LANE)).reshape(OWNERS, 1, LANE)
     code_move = pltpu.make_async_copy(code_ref, code_smem, load_sem.at[3])
@@ -203,7 +202,8 @@
         load.wait()
     code_move.wait()
     ring_end(0, 2)
-    ring_forward(1, 0)
+    ring_end(1, 0)
+    ring_start(1, 1)
 
     row_head = lax.broadcasted_iota(jnp.int32, (GH * QT, GW), 0) // QT
     lane_head = lax.broadcasted_iota(jnp.int32, (GH * QT, GW), 1) // HD
@@ -306,18 +306,21 @@
         for g in PHASES[phase]:
             part_stat[g, delta] = stats[g]
 
-    def rounded(value):
-        return value.astype(jnp.bfloat16).astype(jnp.float32)
-
-    def blend(factors, matrix, blocks):
-        wide = jnp.dot(factors, matrix, preferred_element_type=jnp.float32)
+    def widen(share, at, t):
+        pair = [jnp.broadcast_to(share[:, c : c + 1], (QT, LANE)) for c in (at + 2 * t, at + 2 * t + 1)]
+        return jnp.where(near, pair[0], pair[1])
+
+    def tiles(block):
+        return [block[:, t * LANE : (t + 1) * LANE].astype(jnp.float32) for t in range(GW // LANE)]
+
+    def blend(shares, at, blocks):
         sums = []
-        for at in range(0, factors.shape[0] // QT, SIDE):
-            total = blocks[0] * wide[at * QT : (at + 1) * QT]
+        for t in range(GW // LANE):
+            total = widen(shares[0], at, t) * tiles(blocks[0])[t]
             for d in range(1, SIDE):
-                total = total + blocks[d] * wide[(at + d) * QT : (at + d + 1) * QT]
+                total = total + widen(shares[d], at, t) * tiles(blocks[d])[t]
             sums.append(total)
-        return sums
+        return jnp.concatenate(sums, axis=1).astype(jnp.bfloat16)
 
     def merge_one(g):
         tree_wait(one, g)
@@ -330,61 +333,61 @@
         terms = [
             jnp.exp(jnp.minimum(stat - jnp.where(tag == 1.0, tops[1], tops[0]), 0.0)) for stat, tag in zip(packed, tags)
         ]
-        factors, results = [], []
+        results, inverses = [], []
         for n in range(2):
             kept = [jnp.where(tag == n, term, 0.0) for term, tag in zip(terms, tags)]
             total = jnp.maximum(kept[0] + kept[1] + kept[2] + kept[3], 1e-30)
             results.append(tops[n] + jnp.log(total))
-            for term in kept:
-                share = term / total
-                high = rounded(share)
-                factors.append(jnp.where(stat_lane < LANE // 2, high, pltpu.roll(share - high, LANE // 2, 1)))
+            inverses.append(1.0 / total)
         mid_stat[g] = jnp.where(stat_lane < LANE // 2, results[0], pltpu.roll(results[1], LANE // 2, 1))
-        factors = jnp.concatenate(factors, axis=0).astype(jnp.bfloat16)
+        shares = [
+            term * jnp.where(tag == 1.0, -inverses[1], jnp.where(tag == 0.0, inverses[0], 0.0))
+            for term, tag in zip(terms, tags)
+        ]
 
         def body(j, carry):
             second, third = j >> 2, j & 3
             blocks = [part_ref[g, 0, second, third]] + [near_ref[g, d - 1, second, third] for d in range(1, SIDE)]
-            sums = blend(factors, spread_one[j], [block.astype(jnp.float32) for block in blocks])
-            for n in range(2):
-                mid_ref[g, second, third, n] = sums[n].astype(jnp.bfloat16)
+            turned = [pltpu.roll(share, (LANE - GH * j) & (LANE - 1), 1) for share in shares]
+            for t in range(GW // LANE):
+                totals = [jnp.zeros((QT, LANE), jnp.float32)] * 2
+                for d in range(SIDE):
+                    factor, block = widen(turned[d], 0, t), tiles(blocks[d])[t]
+                    totals = [
+                        totals[0] + jnp.maximum(factor, 0.0) * block,
+                        totals[1] - jnp.minimum(factor, 0.0) * block,
+                    ]
+                for n in range(2):
+                    mid_ref[g, second, third, n, :, t * LANE : (t + 1) * LANE] = totals[n].astype(jnp.bfloat16)
             return carry
 
         lax.fori_loop(0, SIDE * SIDE, body, 0, unroll=4)
         tree_start(two, g)
 
-    def shares_of(packed, span):
+    def shares_of(packed):
         top = jnp.maximum(jnp.maximum(packed[0], packed[1]), jnp.maximum(packed[2], packed[3]))
         terms = [jnp.exp(stat - top) for stat in packed]
         total = terms[0] + terms[1] + terms[2] + terms[3]
-        factors = []
-        for term in terms:
-            share = term / total
-            high = rounded(share)
-            low = pltpu.roll(share - high, span, 1)
-            in_lane = stat_lane & 63
-            factors.append(jnp.where(in_lane < span, high, jnp.where(in_lane < 2 * span, low, 0.0)))
-        return top + jnp.log(total), jnp.concatenate(factors, axis=0).astype(jnp.bfloat16)
+        inverse = 1.0 / total
+        return top + jnp.log(total), [term * inverse for term in terms]
 
     def merge_two(g):
         tree_wait(two, g)
         packed = [mid_stat[g]] + [pltpu.roll(next_stat[g, d - 1], LANE - 16 * d, 1) for d in range(1, SIDE)]
-        late_stat[g], factors = shares_of(packed, 16)
+        late_stat[g], shares = shares_of(packed)
         for third in range(SIDE):
             for n in range(2):
                 blocks = [mid_ref[g, 0, third, n]] + [next_ref[g, d - 1, third, n] for d in range(1, SIDE)]
-                sums = blend(factors, spread_two[third * 2 + n], [block.astype(jnp.float32) for block in blocks])
-                late_ref[g, third, n] = sums[0].astype(jnp.bfloat16)
+                late_ref[g, third, n] = blend(shares, n * LANE // 2 + third * GH, blocks)
         tree_start(three, g)
 
     def merge_three(g):
         tree_wait(three, g)
         packed = [late_stat[g]] + [pltpu.roll(last_stat[g, d - 1], LANE - 4 * d, 1) for d in range(1, SIDE)]
-        value, factors = shares_of(packed, 4)
+        value, shares = shares_of(packed)
         for n in range(2):
             blocks = [late_ref[g, 0, n]] + [last_ref[g, d - 1, n] for d in range(1, SIDE)]
-            sums = blend(factors, spread_three[n], [block.astype(jnp.float32) for block in blocks])
-            attended_ref[n * QT : (n + 1) * QT, g * GW : (g + 1) * GW] = sums[0].astype(jnp.bfloat16)
+            attended_ref[n * QT : (n + 1) * QT, g * GW : (g + 1) * GW] = blend(shares, n * LANE // 2, blocks)
 
     def project(phase):
         rows = slice(PHASES[phase][0] * GW, (PHASES[phase][-1] + 1) * GW)
@@ -420,23 +423,17 @@
         lax.fori_loop(0, OWNERS // BATCH, body, 0)
 
     def ring_beside(phase):
-        return {
-            0: [(ring_end, phase, 0), (ring_start, phase, 1)],
-            1: [(ring_forward, phase, 1)],
-            2: [(ring_end, phase, 1), (ring_start, phase, 2)],
-            4: [(ring_forward, phase, 2)],
-        }
+        return {0: [(ring_end, phase, 1), (ring_start, phase, 2)], 4: [(ring_forward, phase, 2)]}
 
     def each(merge, phase):
         for g in PHASES[phase]:
             merge(g)
 
-    run(0, ring_beside(1) | {6: [(ring_start, 2, 0)]})
+    run(0, ring_beside(1) | {5: [(ring_start, 2, 0)], 7: [(ring_end, 2, 0), (ring_start, 2, 1)]})
     ring_end(1, 2)
-    ring_forward(2, 0)
     run(1, ring_beside(2))
+    each(merge_one, 0)
     ring_end(2, 2)
-    each(merge_one, 0)
     run(2, {})
     each(merge_one, 1)
     each(merge_two, 0)
@@ -459,10 +456,6 @@
 
 
 def on_device(queries, keys, values, counts, passage_ids, out_weight):
-    list_len = passage_ids.shape[1]
-    listed = jnp.arange(list_len)[None, :] < counts[:, None]
-    ids = jnp.where(listed, passage_ids, -1).astype(jnp.int32)
-    ids = jnp.pad(ids, ((0, 0), (0, LANE // 2 - list_len)), constant_values=-1).reshape(1, LANE)
     leads = (
         (SIDE, SIDE, SIDE),
         (SIDE - 1, SIDE, SIDE),
@@ -478,19 +471,18 @@
     return pl.pallas_call(
         torus_kernel,
         out_shape=jax.ShapeDtypeStruct((2 * QT, D), jnp.bfloat16),
-        in_specs=[pl.BlockSpec(memory_space=pltpu.VMEM)] * 2 + [pl.BlockSpec(memory_space=pl.ANY)] * 3,
+        in_specs=[pl.BlockSpec(memory_space=pltpu.SMEM)]
+        + [pl.BlockSpec(memory_space=pltpu.VMEM)] * 2
+        + [pl.BlockSpec(memory_space=pl.ANY)] * 3,
         out_specs=pl.BlockSpec(memory_space=pltpu.VMEM),
         scratch_shapes=blocks
         + [
             pltpu.VMEM(keys.shape, jnp.bfloat16),
             pltpu.VMEM(values.shape, jnp.bfloat16),
             pltpu.VMEM((D, D), jnp.bfloat16),
-            pltpu.VMEM((SIDE, SIDE, SIDE, 1, LANE), jnp.int32),
+            pltpu.VMEM((SIDE, SIDE, SIDE, 2, LANE), jnp.int32),
             pltpu.VMEM((OWNERS, 1, LANE), jnp.int32),
             pltpu.SMEM((OWNERS, 1, LANE), jnp.int32),
-            pltpu.VMEM((SIDE * SIDE, LANE, GW), jnp.bfloat16),
-            pltpu.VMEM((2 * SIDE, LANE, GW), jnp.bfloat16),
-            pltpu.VMEM((2, LANE, GW), jnp.bfloat16),
             pltpu.VMEM((2 * QT, D), jnp.bfloat16),
             pltpu.VMEM((2 * QT, D), jnp.float32),
             pltpu.SemaphoreType.DMA((4,)),
@@ -508,7 +500,7 @@
         ),
         cost_estimate=pl.CostEstimate(flops=40 * 10**9, bytes_accessed=20 * 2**20, transcendentals=4 * 10**6),
         name="torus",
-    )(ids, queries, keys, values, out_weight)
+    )(counts, passage_ids, queries, keys, values, out_weight)
 
 
 def solution(mesh):

time: 130 us -> 120 us (0.923)
  Pallas kernels: 127 us -> 118 us
    pallas_call x1, Pallas kernels: 127 us -> 118 us  [on_device(): pl.pallas_call(torus_kernel, out_shape=jax.ShapeDtypeStruct((2 * QT, D),...]
where the time goes in v4:
time: 120 us; the launch traced here: 119 us
  Pallas kernels  118 us (98%)
  local copies, waits for them, and re-layouts  1.57 us (1%)
    pallas_call x1, Pallas kernels, on_device(): pl.pallas_call(torus_kernel, out_shape=jax.ShapeDtypeStruct((2 * QT, D),...  118 us

profile of v4, /device:TPU:0, one launch (start us, length us, event | category | flops | bytes accessed | tf_op | source)
XLA Modules:
  0.0 119.5 jit_solution(10005963875923386213)
XLA Ops:
  0.0 117.9 %torus.1 = bf16[32,2048]{1,0:T(8,128)(2,1)} custom-call(s32[2]{0:T(128)} %counts_ref.1, s32[2,28]{1,0:T(2,128)} %ids_ref.1, bf16[32,2048]{1,0:T(8,128)(2,1)} %mine_ref.1, bf16[16,64,2048]{2,1,0:T(8,128)(2,1)} %k_hbm.1, bf16[16,64,2048]{2,1,0:T(8,128)(2,1)} %v_hbm.1, bf16[1024,2048]{1,0:T(8,128)(2,1)} %w_hbm.1), custom_call_target="tpu_custom_call" | custom-call | flops 40000000000 | bytes 20971520 | tf_op jit(solution)/shard_map/torus/pallas_call | solution.py:471
  117.9 1.6 %copy.8 = bf16[32,2048]{1,0:T(8,128)(2,1)} copy(bf16[32,2048]{1,0:T(8,128)(2,1)} %torus.1) | data formatting | bytes 262144

commit v5 on v4

--- a/solution.py
+++ b/solution.py
@@ -194,16 +194,11 @@
     code_ref[...] = jnp.broadcast_to(code, (OWNERS, LANE)).reshape(OWNERS, 1, LANE)
     code_move = pltpu.make_async_copy(code_ref, code_smem, load_sem.at[3])
     code_move.start()
-    ring_forward(0, 2)
-    ring_start(1, 0)
     w_home.start()
     w_give.start()
     for load in loads:
         load.wait()
     code_move.wait()
-    ring_end(0, 2)
-    ring_end(1, 0)
-    ring_start(1, 1)
 
     row_head = lax.broadcasted_iota(jnp.int32, (GH * QT, GW), 0) // QT
     lane_head = lax.broadcasted_iota(jnp.int32, (GH * QT, GW), 1) // HD
@@ -249,14 +244,27 @@
     stride = {"y": SIDE * SIDE, "x": SIDE, "z": 1}
 
     def attend(phase, b):
-        delta, part_half = ((b >> 1) + 1) & 3, b & 1
+        turn, part_half = b >> 1, b & 1
         items = [(n, g) for n in range(BATCH) for g in PHASES[phase]]
-        slots, tags, scores, weights = {}, {}, {}, {}
-        lane = stat_lane - part_half * (BATCH * GH)
-        stats = {g: part_stat[g, delta] for g in PHASES[phase]}
+        slots, tags, scores, weights, stats = {}, {}, {}, {}, {}
+        if phase < 2:
+            third = turn + (turn >> 1) * (1 - 2 * (turn & 1))
+            lane = stat_lane - third * GH
+            for n, g in items:
+                stats[n // SIDE, g] = part_stat[g, part_half * 2 + n // SIDE]
+        else:
+            delta = (turn + 1) & 3
+            lane = stat_lane - part_half * (BATCH * GH)
+            for g in PHASES[phase]:
+                stats[0, g] = part_stat[g, delta]
 
         def place(n):
+            if phase < 2:
+                return part_half * 2 + n // SIDE, n % SIDE, third
             return delta, part_half * 2 + n // SIDE, n % SIDE
+
+        def home(n):
+            return (n // SIDE, (n % SIDE) * SIDE) if phase < 2 else (0, n)
 
         for n, g in items:
             told = code_smem[sum(at * stride[axis] for axis, at in zip(order_of(g), place(n))), 0, 0]
@@ -279,9 +287,11 @@
             shaped = jnp.exp(values - peak)
             total = jnp.sum(shaped, axis=1, keepdims=True)
             lse = peak + jnp.log(total * jnp.where(first == second, 0.5, 1.0))
+            tile, at = home(n)
+            stat = stats[tile, g]
             for h in range(GH):
-                stats[g] = jnp.where(lane == n * GH + h, lse[h * QT : (h + 1) * QT], stats[g])
-            stats[g] = jnp.where(((lane - LANE // 2) >> 2) == n, tags[n, g], stats[g])
+                stat = jnp.where(lane == at * GH + h, lse[h * QT : (h + 1) * QT], stat)
+            stats[tile, g] = jnp.where(((lane - LANE // 2) >> 2) == at, tags[n, g], stat)
             weights[n, g] = (shaped.astype(jnp.bfloat16), 1.0 / total)
 
         def apply(n, g):
@@ -303,8 +313,8 @@
                 weigh(*items[at - 2])
             if 4 <= at:
                 apply(*items[at - 4])
-        for g in PHASES[phase]:
-            part_stat[g, delta] = stats[g]
+        for (tile, g), stat in stats.items():
+            part_stat[g, part_half * 2 + tile if phase < 2 else delta] = stat
 
     def widen(share, at, t):
         pair = [jnp.broadcast_to(share[:, c : c + 1], (QT, LANE)) for c in (at + 2 * t, at + 2 * t + 1)]
@@ -399,16 +409,13 @@
         else:
             out_ref[...] = (sum_ref[...] + product).astype(jnp.bfloat16)
 
-    def run(phase, beside):
-        def send(by):
+    def send(phase, *offsets):
+        for by in offsets:
             for g in PHASES[phase]:
                 for copy in one(g, by):
                     copy.start()
 
-        beside = {at: list(acts) for at, acts in beside.items()}
-        for by in range(1, SIDE):
-            beside.setdefault(2 * by - 1, []).insert(0, (send, by))
-
+    def run(phase, beside):
         def body(b, carry):
             attend(phase, b)
             for at, acts in beside.items():
@@ -422,19 +429,35 @@
 
         lax.fori_loop(0, OWNERS // BATCH, body, 0)
 
-    def ring_beside(phase):
-        return {0: [(ring_end, phase, 1), (ring_start, phase, 2)], 4: [(ring_forward, phase, 2)]}
-
     def each(merge, phase):
         for g in PHASES[phase]:
             merge(g)
 
-    run(0, ring_beside(1) | {5: [(ring_start, 2, 0)], 7: [(ring_end, 2, 0), (ring_start, 2, 1)]})
-    ring_end(1, 2)
-    run(1, ring_beside(2))
+    run(
+        0,
+        {
+            1: [(ring_forward, 0, 2), (ring_start, 1, 0)],
+            3: [(ring_end, 1, 0), (ring_start, 1, 1)],
+            5: [(ring_end, 0, 2)],
+            6: [(ring_end, 1, 1), (ring_start, 1, 2)],
+        },
+    )
+    send(0, 2, 1, 3)
+    run(
+        1,
+        {
+            0: [(ring_start, 2, 0)],
+            1: [(ring_forward, 1, 2)],
+            2: [(ring_end, 2, 0), (ring_start, 2, 1)],
+            4: [(ring_end, 2, 1), (ring_start, 2, 2)],
+            5: [(ring_end, 1, 2)],
+            7: [(ring_forward, 2, 2)],
+        },
+    )
+    send(1, 2, 1, 3)
     each(merge_one, 0)
     ring_end(2, 2)
-    run(2, {})
+    run(2, {1: [(send, 2, 1)], 3: [(send, 2, 2)], 5: [(send, 2, 3)]})
     each(merge_one, 1)
     each(merge_two, 0)
     each(merge_one, 2)

time: 120 us -> 114 us (0.950)
  Pallas kernels: 118 us -> 112 us
    pallas_call x1, Pallas kernels: 118 us -> 112 us  [on_device(): pl.pallas_call(torus_kernel, out_shape=jax.ShapeDtypeStruct((2 * QT, D),...]
where the time goes in v5:
time: 114 us
  Pallas kernels  112 us (98%)
  local copies, waits for them, and re-layouts  1.57 us (1%)
    pallas_call x1, Pallas kernels, on_device(): pl.pallas_call(torus_kernel, out_shape=jax.ShapeDtypeStruct((2 * QT, D),...  112 us

profile of v5, /device:TPU:0, one launch (start us, length us, event | category | flops | bytes accessed | tf_op | source)
XLA Modules:
  0.0 113.7 jit_solution(20943087402886102)
XLA Ops:
  0.0 112.1 %torus.1 = bf16[32,2048]{1,0:T(8,128)(2,1)} custom-call(s32[2]{0:T(128)} %counts_ref.1, s32[2,28]{1,0:T(2,128)} %ids_ref.1, bf16[32,2048]{1,0:T(8,128)(2,1)} %mine_ref.1, bf16[16,64,2048]{2,1,0:T(8,128)(2,1)} %k_hbm.1, bf16[16,64,2048]{2,1,0:T(8,128)(2,1)} %v_hbm.1, bf16[1024,2048]{1,0:T(8,128)(2,1)} %w_hbm.1), custom_call_target="tpu_custom_call" | custom-call | flops 40000000000 | bytes 20971520 | tf_op jit(solution)/shard_map/torus/pallas_call | solution.py:494
  112.1 1.6 %copy.8 = bf16[32,2048]{1,0:T(8,128)(2,1)} copy(bf16[32,2048]{1,0:T(8,128)(2,1)} %torus.1) | data formatting | bytes 262144

commit v6 on v5

--- a/solution.py
+++ b/solution.py
@@ -17,7 +17,8 @@
 SIDE = 4
 OWNERS = SIDE * SIDE * SIDE
 PHASES = ((0, 1, 2), (3, 4, 5), (6, 7))
-BATCH = 8
+BATCH = 4
+
 DEAD = -1e30
 ORDERS = (("x", "y", "z"), ("y", "z", "x"), ("z", "x", "y"))
 MESH = pl.DeviceIdType.MESH
@@ -27,7 +28,7 @@
     counts_ref, ids_ref, mine_ref, k_hbm, v_hbm, w_hbm, out_ref,
     q_ref, part_ref, near_ref, mid_ref, next_ref, late_ref, last_ref,
     part_stat, near_stat, mid_stat, next_stat, late_stat, last_stat,
-    k_ref, v_ref, w_ref, list_ref, code_ref, code_smem, attended_ref, sum_ref,
+    k_ref, v_ref, w_ref, list_ref, code_ref, code_smem, score_ref, weight_ref, inverse_ref, attended_ref, sum_ref,
     load_sem, home_sem, list_send, list_recv, w_sem, ring_send, ring_recv, tree_send, tree_recv,
 ):
     me = lax.axis_index("dev")
@@ -202,7 +203,7 @@
 
     row_head = lax.broadcasted_iota(jnp.int32, (GH * QT, GW), 0) // QT
     lane_head = lax.broadcasted_iota(jnp.int32, (GH * QT, GW), 1) // HD
-    diag = (row_head == lane_head).astype(jnp.float32).astype(jnp.bfloat16)
+    diag = jnp.where(row_head == lane_head, 0.125, 0.0).astype(jnp.bfloat16)
     stat_lane = lax.broadcasted_iota(jnp.int32, (QT, LANE), 1)
     near = stat_lane < HD
 
@@ -243,78 +244,102 @@
 
     stride = {"y": SIDE * SIDE, "x": SIDE, "z": 1}
 
+    def place(phase, b, n):
+        turn, quarter = b >> 2, b & 3
+        if phase < 2:
+            return quarter, n, turn + (turn >> 1) * (1 - 2 * (turn & 1))
+        return (turn + 1) & 3, quarter, n
+
+    def told(phase, b, n, g):
+        return code_smem[sum(at * stride[axis] for axis, at in zip(order_of(g), place(phase, b, n))), 0, 0]
+
+    def passages(code):
+        code = jnp.maximum(code, 0)
+        return code & 1, (code >> 1) & 15, (code >> 5) & 15
+
+    def items_of(phase):
+        return [(n, g) for n in range(BATCH) for g in PHASES[phase]]
+
+    def score(phase, b, at):
+        n, g = items_of(phase)[at]
+        which, first, second = passages(told(phase, b, n, g))
+        cols = slice(g * GW, (g + 1) * GW)
+        spot = place(phase, b, n)
+        q = jnp.where(which > 0, q_ref[(g, *spot, slice(QT, 2 * QT))], q_ref[(g, *spot, slice(0, QT))])
+        lhs = jnp.concatenate([q] * GH, axis=0) * diag
+        k = jnp.concatenate([k_ref[first, :, cols], k_ref[second, :, cols]], axis=0)
+        score_ref[at] = lax.dot_general(lhs, k, (((1,), (1,)), ((), ())), preferred_element_type=jnp.float32)
+
+    def weigh(phase, b, at, packed):
+        n, g = items_of(phase)[at]
+        code = told(phase, b, n, g)
+        which, first, second = passages(code)
+        values = score_ref[at]
+        peak = jnp.max(values, axis=1, keepdims=True)
+        shaped = jnp.exp(values - peak)
+        total = jnp.sum(shaped, axis=1, keepdims=True)
+        weight_ref[at] = shaped.astype(jnp.bfloat16)
+        rows = [slice(h * QT, (h + 1) * QT) for h in range(GH)]
+        for t in range(GW // LANE):
+            pair = jnp.where(near, total[rows[2 * t]], total[rows[2 * t + 1]])
+            inverse_ref[at, :, t * LANE : (t + 1) * LANE] = 1.0 / pair
+        lane, peaks, totals, tags = packed[g]
+        spot = n * SIDE if phase < 2 else n
+        for h in range(GH):
+            here = lane == spot * GH + h
+            peaks = jnp.where(here, peak[rows[h]], peaks)
+            totals = jnp.where(here, total[rows[h]], totals)
+        share = jnp.where(first == second, 0.5, 1.0)
+        totals = jnp.where((lane >> 2) == spot, totals * share, totals)
+        tag = jnp.where(code < 0, -1.0, jnp.where(which > 0, 1.0, 0.0))
+        tags = jnp.where(((lane - LANE // 2) >> 2) == spot, tag, tags)
+        packed[g] = (lane, peaks, totals, tags)
+
+    def apply(phase, b, at):
+        n, g = items_of(phase)[at]
+        which, first, second = passages(told(phase, b, n, g))
+        cols = slice(g * GW, (g + 1) * GW)
+        v = jnp.concatenate([v_ref[first, :, cols], v_ref[second, :, cols]], axis=0)
+        full = jnp.dot(weight_ref[at], v, preferred_element_type=jnp.float32)
+        for t in range(GW // LANE):
+            lanes = slice(t * LANE, (t + 1) * LANE)
+            a, c = (slice((2 * t + e) * QT, (2 * t + e + 1) * QT) for e in (0, 1))
+            part = jnp.where(near, full[a, lanes], full[c, lanes]) * inverse_ref[at, :, lanes]
+            part_ref[(g, *place(phase, b, n), slice(None), lanes)] = part.astype(jnp.bfloat16)
+
+    def pack_open(phase, b):
+        first, second, third = place(phase, b, 0)
+        lane = stat_lane - (third * GH if phase < 2 else second * GH * SIDE)
+        zero = jnp.zeros((QT, LANE), jnp.float32)
+        return {g: (lane, zero, zero + 1.0, zero) for g in PHASES[phase]}
+
+    def pack_close(phase, b, packed):
+        first, second, third = place(phase, b, 0)
+        for g, (lane, peaks, totals, tags) in packed.items():
+            if phase < 2:
+                mine = (lane & 15) < GH
+            else:
+                mine = ((stat_lane & 63) >> 4) == second
+            value = jnp.where(stat_lane < LANE // 2, peaks + jnp.log(totals), tags)
+            part_stat[g, first] = jnp.where(mine, value, part_stat[g, first])
+
     def attend(phase, b):
-        turn, part_half = b >> 1, b & 1
-        items = [(n, g) for n in range(BATCH) for g in PHASES[phase]]
-        slots, tags, scores, weights, stats = {}, {}, {}, {}, {}
-        if phase < 2:
-            third = turn + (turn >> 1) * (1 - 2 * (turn & 1))
-            lane = stat_lane - third * GH
-            for n, g in items:
-                stats[n // SIDE, g] = part_stat[g, part_half * 2 + n // SIDE]
-        else:
-            delta = (turn + 1) & 3
-            lane = stat_lane - part_half * (BATCH * GH)
-            for g in PHASES[phase]:
-                stats[0, g] = part_stat[g, delta]
-
-        def place(n):
-            if phase < 2:
-                return part_half * 2 + n // SIDE, n % SIDE, third
-            return delta, part_half * 2 + n // SIDE, n % SIDE
-
-        def home(n):
-            return (n // SIDE, (n % SIDE) * SIDE) if phase < 2 else (0, n)
-
-        for n, g in items:
-            told = code_smem[sum(at * stride[axis] for axis, at in zip(order_of(g), place(n))), 0, 0]
-            code = jnp.maximum(told, 0)
-            slots[n, g] = (code & 1, (code >> 1) & 15, (code >> 5) & 15)
-            tags[n, g] = jnp.where(told < 0, -1.0, jnp.where((code & 1) > 0, 1.0, 0.0))
-
-        def score(n, g):
-            which, first, second = slots[n, g]
-            cols = slice(g * GW, (g + 1) * GW)
-            q = jnp.where(which > 0, q_ref[(g, *place(n), slice(QT, 2 * QT))], q_ref[(g, *place(n), slice(0, QT))])
-            lhs = jnp.concatenate([q * jnp.bfloat16(0.125)] * GH, axis=0) * diag
-            k = jnp.concatenate([k_ref[first, :, cols], k_ref[second, :, cols]], axis=0)
-            scores[n, g] = lax.dot_general(lhs, k, (((1,), (1,)), ((), ())), preferred_element_type=jnp.float32)
-
-        def weigh(n, g):
-            which, first, second = slots[n, g]
-            values = scores.pop((n, g))
-            peak = jnp.max(values, axis=1, keepdims=True)
-            shaped = jnp.exp(values - peak)
-            total = jnp.sum(shaped, axis=1, keepdims=True)
-            lse = peak + jnp.log(total * jnp.where(first == second, 0.5, 1.0))
-            tile, at = home(n)
-            stat = stats[tile, g]
-            for h in range(GH):
-                stat = jnp.where(lane == at * GH + h, lse[h * QT : (h + 1) * QT], stat)
-            stats[tile, g] = jnp.where(((lane - LANE // 2) >> 2) == at, tags[n, g], stat)
-            weights[n, g] = (shaped.astype(jnp.bfloat16), 1.0 / total)
-
-        def apply(n, g):
-            which, first, second = slots[n, g]
-            cols = slice(g * GW, (g + 1) * GW)
-            shaped, inverse = weights.pop((n, g))
-            v = jnp.concatenate([v_ref[first, :, cols], v_ref[second, :, cols]], axis=0)
-            full = jnp.dot(shaped, v, preferred_element_type=jnp.float32)
-            for t in range(GW // LANE):
-                lanes = slice(t * LANE, (t + 1) * LANE)
-                a, c = (slice((2 * t + e) * QT, (2 * t + e + 1) * QT) for e in (0, 1))
-                part = jnp.where(near, full[a, lanes] * inverse[a], full[c, lanes] * inverse[c])
-                part_ref[(g, *place(n), slice(None), lanes)] = part.astype(jnp.bfloat16)
-
-        for at in range(len(items) + 4):
-            if at < len(items):
-                score(*items[at])
-            if 2 <= at < len(items) + 2:
-                weigh(*items[at - 2])
-            if 4 <= at:
-                apply(*items[at - 4])
-        for (tile, g), stat in stats.items():
-            part_stat[g, part_half * 2 + tile if phase < 2 else delta] = stat
+        later, latest = jnp.minimum(b + 1, OWNERS // BATCH - 1), jnp.minimum(b + 2, OWNERS // BATCH - 1)
+        packed = pack_open(phase, later)
+        for at in range(len(items_of(phase))):
+            apply(phase, b, at)
+            weigh(phase, later, at, packed)
+            score(phase, latest, at)
+        pack_close(phase, later, packed)
+
+    def prepare(phase):
+        for at in range(len(items_of(phase))):
+            score(phase, 0, at)
+        packed = pack_open(phase, 0)
+        for at in range(len(items_of(phase))):
+            weigh(phase, 0, at, packed)
+            score(phase, 1, at)
+        pack_close(phase, 0, packed)
 
     def widen(share, at, t):
         pair = [jnp.broadcast_to(share[:, c : c + 1], (QT, LANE)) for c in (at + 2 * t, at + 2 * t + 1)]
@@ -416,6 +441,8 @@
                     copy.start()
 
     def run(phase, beside):
+        prepare(phase)
+
         def body(b, carry):
             attend(phase, b)
             for at, acts in beside.items():
@@ -437,9 +464,9 @@
         0,
         {
             1: [(ring_forward, 0, 2), (ring_start, 1, 0)],
-            3: [(ring_end, 1, 0), (ring_start, 1, 1)],
-            5: [(ring_end, 0, 2)],
-            6: [(ring_end, 1, 1), (ring_start, 1, 2)],
+            5: [(ring_end, 1, 0), (ring_start, 1, 1)],
+            9: [(ring_end, 0, 2)],
+            10: [(ring_end, 1, 1), (ring_start, 1, 2)],
         },
     )
     send(0, 2, 1, 3)
@@ -448,16 +475,16 @@
         {
             0: [(ring_start, 2, 0)],
             1: [(ring_forward, 1, 2)],
-            2: [(ring_end, 2, 0), (ring_start, 2, 1)],
-            4: [(ring_end, 2, 1), (ring_start, 2, 2)],
-            5: [(ring_end, 1, 2)],
-            7: [(ring_forward, 2, 2)],
+            4: [(ring_end, 2, 0), (ring_start, 2, 1)],
+            8: [(ring_end, 2, 1), (ring_start, 2, 2)],
+            9: [(ring_end, 1, 2)],
+            14: [(ring_forward, 2, 2)],
         },
     )
     send(1, 2, 1, 3)
     each(merge_one, 0)
     ring_end(2, 2)
-    run(2, {1: [(send, 2, 1)], 3: [(send, 2, 2)], 5: [(send, 2, 3)]})
+    run(2, {3: [(send, 2, 1)], 7: [(send, 2, 2)], 11: [(send, 2, 3)]})
     each(merge_one, 1)
     each(merge_two, 0)
     each(merge_one, 2)
@@ -506,6 +533,9 @@
             pltpu.VMEM((SIDE, SIDE, SIDE, 2, LANE), jnp.int32),
             pltpu.VMEM((OWNERS, 1, LANE), jnp.int32),
             pltpu.SMEM((OWNERS, 1, LANE), jnp.int32),
+            pltpu.VMEM((3 * BATCH, GH * QT, 2 * PT), jnp.float32),
+            pltpu.VMEM((3 * BATCH, GH * QT, 2 * PT), jnp.bfloat16),
+            pltpu.VMEM((3 * BATCH, QT, GW), jnp.float32),
             pltpu.VMEM((2 * QT, D), jnp.bfloat16),
             pltpu.VMEM((2 * QT, D), jnp.float32),
             pltpu.SemaphoreType.DMA((4,)),

time: 114 us -> 112 us (0.982)
  Pallas kernels: 112 us -> 110 us
    pallas_call x1, Pallas kernels: 112 us -> 110 us  [on_device(): pl.pallas_call(torus_kernel, out_shape=jax.ShapeDtypeStruct((2 * QT, D),...]
where the time goes in v6:
time: 112 us
  Pallas kernels  110 us (98%)
  local copies, waits for them, and re-layouts  1.57 us (1%)
    pallas_call x1, Pallas kernels, on_device(): pl.pallas_call(torus_kernel, out_shape=jax.ShapeDtypeStruct((2 * QT, D),...  110 us

profile of v6, /device:TPU:0, one launch (start us, length us, event | category | flops | bytes accessed | tf_op | source)
XLA Modules:
  0.0 111.8 jit_solution(6242922631153533943)
XLA Ops:
  0.0 110.2 %torus.1 = bf16[32,2048]{1,0:T(8,128)(2,1)} custom-call(s32[2]{0:T(128)} %counts_ref.1, s32[2,28]{1,0:T(2,128)} %ids_ref.1, bf16[32,2048]{1,0:T(8,128)(2,1)} %mine_ref.1, bf16[16,64,2048]{2,1,0:T(8,128)(2,1)} %k_hbm.1, bf16[16,64,2048]{2,1,0:T(8,128)(2,1)} %v_hbm.1, bf16[1024,2048]{1,0:T(8,128)(2,1)} %w_hbm.1), custom_call_target="tpu_custom_call" | custom-call | flops 40000000000 | bytes 20971520 | tf_op jit(solution)/shard_map/torus/pallas_call | solution.py:521
  110.2 1.6 %copy.8 = bf16[32,2048]{1,0:T(8,128)(2,1)} copy(bf16[32,2048]{1,0:T(8,128)(2,1)} %torus.1) | data formatting | bytes 262144

commit v7 on v6

--- a/solution.py
+++ b/solution.py
@@ -469,13 +469,14 @@
             10: [(ring_end, 1, 1), (ring_start, 1, 2)],
         },
     )
-    send(0, 2, 1, 3)
     run(
         1,
         {
             0: [(ring_start, 2, 0)],
-            1: [(ring_forward, 1, 2)],
+            1: [(ring_forward, 1, 2), (send, 0, 2)],
+            3: [(send, 0, 1)],
             4: [(ring_end, 2, 0), (ring_start, 2, 1)],
+            5: [(send, 0, 3)],
             8: [(ring_end, 2, 1), (ring_start, 2, 2)],
             9: [(ring_end, 1, 2)],
             14: [(ring_forward, 2, 2)],
@@ -484,23 +485,22 @@
     send(1, 2, 1, 3)
     each(merge_one, 0)
     ring_end(2, 2)
-    run(2, {3: [(send, 2, 1)], 7: [(send, 2, 2)], 11: [(send, 2, 3)]})
-    each(merge_one, 1)
-    each(merge_two, 0)
-    each(merge_one, 2)
-    each(merge_two, 1)
+    run(2, {3: [(send, 2, 1)], 7: [(send, 2, 2)], 10: [(each, merge_two, 0)], 11: [(send, 2, 3)]})
     each(merge_three, 0)
     w_home.wait()
     w_give.wait_send()
     w_take.wait_recv()
     project(0)
-    each(merge_two, 2)
-    each(merge_three, 1)
-    project(1)
+    each(merge_one, 1)
+    each(merge_one, 2)
+    each(merge_two, 1)
     ring_sent()
     for stage in range(3):
         for by in range(1, SIDE):
             list_copy(stage, by).wait_send()
+    each(merge_two, 2)
+    each(merge_three, 1)
+    project(1)
     each(merge_three, 2)
     project(2)
 

time: 112 us -> 117 us (1.045)
  Pallas kernels: 110 us -> 116 us
    pallas_call x1, Pallas kernels: 110 us -> 116 us  [on_device(): pl.pallas_call(torus_kernel, out_shape=jax.ShapeDtypeStruct((2 * QT, D),...]
where the time goes in v7:
time: 117 us
  Pallas kernels  116 us (99%)
  local copies, waits for them, and re-layouts  1.57 us (1%)
    pallas_call x1, Pallas kernels, on_device(): pl.pallas_call(torus_kernel, out_shape=jax.ShapeDtypeStruct((2 * QT, D),...  116 us

profile of v7, /device:TPU:0, one launch (start us, length us, event | category | flops | bytes accessed | tf_op | source)
XLA Modules:
  0.0 117.2 jit_solution(8746513022671930925)
XLA Ops:
  0.0 115.6 %torus.1 = bf16[32,2048]{1,0:T(8,128)(2,1)} custom-call(s32[2]{0:T(128)} %counts_ref.1, s32[2,28]{1,0:T(2,128)} %ids_ref.1, bf16[32,2048]{1,0:T(8,128)(2,1)} %mine_ref.1, bf16[16,64,2048]{2,1,0:T(8,128)(2,1)} %k_hbm.1, bf16[16,64,2048]{2,1,0:T(8,128)(2,1)} %v_hbm.1, bf16[1024,2048]{1,0:T(8,128)(2,1)} %w_hbm.1), custom_call_target="tpu_custom_call" | custom-call | flops 40000000000 | bytes 20971520 | tf_op jit(solution)/shard_map/torus/pallas_call | solution.py:521
  115.7 1.6 %copy.8 = bf16[32,2048]{1,0:T(8,128)(2,1)} copy(bf16[32,2048]{1,0:T(8,128)(2,1)} %torus.1) | data formatting | bytes 262144

commit v8 on v6

--- a/solution.py
+++ b/solution.py
@@ -27,7 +27,7 @@
 def torus_kernel(
     counts_ref, ids_ref, mine_ref, k_hbm, v_hbm, w_hbm, out_ref,
     q_ref, part_ref, near_ref, mid_ref, next_ref, late_ref, last_ref,
-    part_stat, near_stat, mid_stat, next_stat, late_stat, last_stat,
+    part_stat, mid_stat, late_stat,
     k_ref, v_ref, w_ref, list_ref, code_ref, code_smem, score_ref, weight_ref, inverse_ref, attended_ref, sum_ref,
     load_sem, home_sem, list_send, list_recv, w_sem, ring_send, ring_recv, tree_send, tree_recv,
 ):
@@ -83,8 +83,8 @@
         return pltpu.make_async_remote_copy(
             src_ref=source,
             dst_ref=ring_block(g, stage, at, whole),
-            send_sem=ring_send.at[g, stage, kind],
-            recv_sem=ring_recv.at[g, stage, kind],
+            send_sem=ring_send.at[g, stage],
+            recv_sem=ring_recv.at[g, stage + kind if stage == 2 else stage],
             device_id=line[order_of(g)[stage]][by],
             device_id_type=MESH,
         )
@@ -93,8 +93,8 @@
         return pltpu.make_async_remote_copy(
             src_ref=ring_block(g, stage, at, rows),
             dst_ref=ring_block(g, stage, 2, rows),
-            send_sem=ring_send.at[g, stage, 2 + kind],
-            recv_sem=ring_recv.at[g, stage, 2 + kind],
+            send_sem=ring_send.at[g, stage],
+            recv_sem=ring_recv.at[g, 4],
             device_id=line[order_of(g)[stage]][by],
             device_id_type=MESH,
         )
@@ -107,24 +107,27 @@
     def ring_forward(phase, stage):
         for kind, by, at, rows in both:
             for g in PHASES[phase]:
-                ring_own(g, stage, kind, by, at).wait_recv()
+                taken(ring_block(g, stage, at, whole), ring_recv.at[g, stage + kind])
                 ring_pass(g, stage, kind, by, at, rows).start()
+
+    def taken(ref, sem):
+        pltpu.make_async_copy(ref, ref, sem).wait()
+
+    def ring_all(g, stage):
+        spot = [pl.ds(0, SIDE) if n < stage else pl.ds(1, 3) if n == stage else 0 for n in range(3)]
+        return q_ref.at[g, spot[0], spot[1], spot[2]]
 
     def ring_end(phase, stage):
         for g in PHASES[phase]:
-            for kind, by, at, rows in sends(stage):
-                if stage == 2:
-                    ring_pass(g, stage, kind, by, at, rows).wait_recv()
-                else:
-                    ring_own(g, stage, kind, by, at).wait_recv()
+            if stage == 2:
+                taken(ring_block(g, stage, 2, whole), ring_recv.at[g, 4])
+            else:
+                taken(ring_all(g, stage), ring_recv.at[g, stage])
 
     def ring_sent():
         for g in range(GROUPS):
             for stage in range(3):
-                for kind, by, at, rows in sends(stage):
-                    ring_own(g, stage, kind, by, at).wait_send()
-                    if stage == 2:
-                        ring_pass(g, stage, kind, by, at, rows).wait_send()
+                taken(ring_all(g, stage), ring_send.at[g, stage])
 
     def list_copy(stage, by):
         order = ("x", "y", "z")
@@ -207,40 +210,36 @@
     stat_lane = lax.broadcasted_iota(jnp.int32, (QT, LANE), 1)
     near = stat_lane < HD
 
-    def tree(sources, targets, g, stage, by):
-        return [
-            pltpu.make_async_remote_copy(
-                src_ref=source,
-                dst_ref=target,
-                send_sem=tree_send.at[stage, g, by, n],
-                recv_sem=tree_recv.at[stage, g, by, n],
-                device_id=line[order_of(g)[stage]][by],
-                device_id_type=MESH,
-            )
-            for n, (source, target) in enumerate(zip(sources, targets))
-        ]
-
-    def one(g, by):
-        return tree(
-            (part_ref.at[g, by], part_stat.at[g, by]), (near_ref.at[g, by - 1], near_stat.at[g, by - 1]), g, 0, by
-        )
-
-    def two(g, by):
-        return tree((mid_ref.at[g, by], mid_stat.at[g]), (next_ref.at[g, by - 1], next_stat.at[g, by - 1]), g, 1, by)
-
-    def three(g, by):
-        return tree((late_ref.at[g, by], late_stat.at[g]), (last_ref.at[g, by - 1], last_stat.at[g, by - 1]), g, 2, by)
-
-    def tree_start(stage, g):
-        for by in range(1, SIDE):
-            for copy in stage(g, by):
-                copy.start()
+    trees = ((part_ref, near_ref), (mid_ref, next_ref), (late_ref, last_ref))
+
+    def tree_start(stage, g, by):
+        source, target = trees[stage]
+        pltpu.make_async_remote_copy(
+            src_ref=source.at[g, by],
+            dst_ref=target.at[g, by - 1],
+            send_sem=tree_send.at[stage, g],
+            recv_sem=tree_recv.at[stage, g],
+            device_id=line[order_of(g)[stage]][by],
+            device_id_type=MESH,
+        ).start()
 
     def tree_wait(stage, g):
-        for by in range(1, SIDE):
-            for copy in stage(g, by):
-                copy.wait_send()
-                copy.wait_recv()
+        target = trees[stage][1]
+        taken(target.at[g], tree_send.at[stage, g])
+        taken(target.at[g], tree_recv.at[stage, g])
+
+    def put_stat(ref, g, by, value):
+        high = value.astype(jnp.bfloat16).astype(jnp.float32)
+        rest = value - high
+        middle = rest.astype(jnp.bfloat16).astype(jnp.float32)
+        blocks = ref.shape[2] - 2
+        ref[g, by, blocks] = jnp.concatenate([high, middle], axis=1).astype(jnp.bfloat16)
+        ref[g, by, blocks + 1] = jnp.concatenate([rest - middle, jnp.zeros_like(high)], axis=1).astype(jnp.bfloat16)
+
+    def get_stat(ref, g, d):
+        blocks = ref.shape[2] - 2
+        first = ref[g, d - 1, blocks].astype(jnp.float32)
+        return first[:, :LANE] + first[:, LANE:] + ref[g, d - 1, blocks + 1, :, :LANE].astype(jnp.float32)
 
     stride = {"y": SIDE * SIDE, "x": SIDE, "z": 1}
 
@@ -249,6 +248,9 @@
         if phase < 2:
             return quarter, n, turn + (turn >> 1) * (1 - 2 * (turn & 1))
         return (turn + 1) & 3, quarter, n
+
+    def block_of(g, spot):
+        return g, spot[0], spot[1] * SIDE + spot[2]
 
     def told(phase, b, n, g):
         return code_smem[sum(at * stride[axis] for axis, at in zip(order_of(g), place(phase, b, n))), 0, 0]
@@ -305,7 +307,7 @@
             lanes = slice(t * LANE, (t + 1) * LANE)
             a, c = (slice((2 * t + e) * QT, (2 * t + e + 1) * QT) for e in (0, 1))
             part = jnp.where(near, full[a, lanes], full[c, lanes]) * inverse_ref[at, :, lanes]
-            part_ref[(g, *place(phase, b, n), slice(None), lanes)] = part.astype(jnp.bfloat16)
+            part_ref[(*block_of(g, place(phase, b, n)), slice(None), lanes)] = part.astype(jnp.bfloat16)
 
     def pack_open(phase, b):
         first, second, third = place(phase, b, 0)
@@ -358,8 +360,8 @@
         return jnp.concatenate(sums, axis=1).astype(jnp.bfloat16)
 
     def merge_one(g):
-        tree_wait(one, g)
-        packed = [part_stat[g, 0]] + [near_stat[g, d - 1] for d in range(1, SIDE)]
+        tree_wait(0, g)
+        packed = [part_stat[g, 0]] + [get_stat(near_ref, g, d) for d in range(1, SIDE)]
         tags = [pltpu.roll(stat, LANE // 2, 1) for stat in packed]
         tops = []
         for n in range(2):
@@ -374,7 +376,7 @@
             total = jnp.maximum(kept[0] + kept[1] + kept[2] + kept[3], 1e-30)
             results.append(tops[n] + jnp.log(total))
             inverses.append(1.0 / total)
-        mid_stat[g] = jnp.where(stat_lane < LANE // 2, results[0], pltpu.roll(results[1], LANE // 2, 1))
+        stat = jnp.where(stat_lane < LANE // 2, results[0], pltpu.roll(results[1], LANE // 2, 1))
         shares = [
             term * jnp.where(tag == 1.0, -inverses[1], jnp.where(tag == 0.0, inverses[0], 0.0))
             for term, tag in zip(terms, tags)
@@ -382,7 +384,7 @@
 
         def body(j, carry):
             second, third = j >> 2, j & 3
-            blocks = [part_ref[g, 0, second, third]] + [near_ref[g, d - 1, second, third] for d in range(1, SIDE)]
+            blocks = [part_ref[g, 0, j]] + [near_ref[g, d - 1, j] for d in range(1, SIDE)]
             turned = [pltpu.roll(share, (LANE - GH * j) & (LANE - 1), 1) for share in shares]
             for t in range(GW // LANE):
                 totals = [jnp.zeros((QT, LANE), jnp.float32)] * 2
@@ -393,11 +395,14 @@
                         totals[1] - jnp.minimum(factor, 0.0) * block,
                     ]
                 for n in range(2):
-                    mid_ref[g, second, third, n, :, t * LANE : (t + 1) * LANE] = totals[n].astype(jnp.bfloat16)
+                    mid_ref[g, second, third * 2 + n, :, t * LANE : (t + 1) * LANE] = totals[n].astype(jnp.bfloat16)
             return carry
 
         lax.fori_loop(0, SIDE * SIDE, body, 0, unroll=4)
-        tree_start(two, g)
+        mid_stat[g] = stat
+        for by in range(1, SIDE):
+            put_stat(mid_ref, g, by, stat)
+            tree_start(1, g, by)
 
     def shares_of(packed):
         top = jnp.maximum(jnp.maximum(packed[0], packed[1]), jnp.maximum(packed[2], packed[3]))
@@ -407,18 +412,21 @@
         return top + jnp.log(total), [term * inverse for term in terms]
 
     def merge_two(g):
-        tree_wait(two, g)
-        packed = [mid_stat[g]] + [pltpu.roll(next_stat[g, d - 1], LANE - 16 * d, 1) for d in range(1, SIDE)]
-        late_stat[g], shares = shares_of(packed)
+        tree_wait(1, g)
+        packed = [mid_stat[g]] + [pltpu.roll(get_stat(next_ref, g, d), LANE - 16 * d, 1) for d in range(1, SIDE)]
+        stat, shares = shares_of(packed)
         for third in range(SIDE):
             for n in range(2):
-                blocks = [mid_ref[g, 0, third, n]] + [next_ref[g, d - 1, third, n] for d in range(1, SIDE)]
+                blocks = [mid_ref[g, 0, third * 2 + n]] + [next_ref[g, d - 1, third * 2 + n] for d in range(1, SIDE)]
                 late_ref[g, third, n] = blend(shares, n * LANE // 2 + third * GH, blocks)
-        tree_start(three, g)
+        late_stat[g] = stat
+        for by in range(1, SIDE):
+            put_stat(late_ref, g, by, stat)
+            tree_start(2, g, by)
 
     def merge_three(g):
-        tree_wait(three, g)
-        packed = [late_stat[g]] + [pltpu.roll(last_stat[g, d - 1], LANE - 4 * d, 1) for d in range(1, SIDE)]
+        tree_wait(2, g)
+        packed = [late_stat[g]] + [pltpu.roll(get_stat(last_ref, g, d), LANE - 4 * d, 1) for d in range(1, SIDE)]
         value, shares = shares_of(packed)
         for n in range(2):
             blocks = [late_ref[g, 0, n]] + [last_ref[g, d - 1, n] for d in range(1, SIDE)]
@@ -437,8 +445,8 @@
     def send(phase, *offsets):
         for by in offsets:
             for g in PHASES[phase]:
-                for copy in one(g, by):
-                    copy.start()
+                put_stat(part_ref, g, by, part_stat[g, by])
+                tree_start(0, g, by)
 
     def run(phase, beside):
         prepare(phase)
@@ -485,8 +493,8 @@
     each(merge_one, 0)
     ring_end(2, 2)
     run(2, {3: [(send, 2, 1)], 7: [(send, 2, 2)], 11: [(send, 2, 3)]})
+    each(merge_two, 0)
     each(merge_one, 1)
-    each(merge_two, 0)
     each(merge_one, 2)
     each(merge_two, 1)
     each(merge_three, 0)
@@ -506,17 +514,11 @@
 
 
 def on_device(queries, keys, values, counts, passage_ids, out_weight):
-    leads = (
-        (SIDE, SIDE, SIDE),
-        (SIDE - 1, SIDE, SIDE),
-        (SIDE, SIDE, 2),
-        (SIDE - 1, SIDE, 2),
-        (SIDE, 2),
-        (SIDE - 1, 2),
-    )
     blocks = [pltpu.VMEM((GROUPS, SIDE, SIDE, SIDE, 2 * QT, GW), jnp.bfloat16)]
-    blocks += [pltpu.VMEM((GROUPS, *lead, QT, GW), jnp.bfloat16) for lead in leads]
-    for lead in ((SIDE,), (SIDE - 1,), (), (SIDE - 1,), (), (SIDE - 1,)):
+    for count in (SIDE * SIDE, 2 * SIDE, 2):
+        for lead in (SIDE, SIDE - 1):
+            blocks.append(pltpu.VMEM((GROUPS, lead, count + 2, QT, GW), jnp.bfloat16))
+    for lead in ((SIDE,), (), ()):
         blocks.append(pltpu.VMEM((GROUPS, *lead, QT, LANE), jnp.float32))
     return pl.pallas_call(
         torus_kernel,
@@ -543,10 +545,10 @@
             pltpu.SemaphoreType.DMA((3, SIDE)),
             pltpu.SemaphoreType.DMA((3, SIDE)),
             pltpu.SemaphoreType.DMA((2,)),
-            pltpu.SemaphoreType.DMA((GROUPS, 3, 4)),
-            pltpu.SemaphoreType.DMA((GROUPS, 3, 4)),
-            pltpu.SemaphoreType.DMA((3, GROUPS, SIDE, 2)),
-            pltpu.SemaphoreType.DMA((3, GROUPS, SIDE, 2)),
+            pltpu.SemaphoreType.DMA((GROUPS, 3)),
+            pltpu.SemaphoreType.DMA((GROUPS, 5)),
+            pltpu.SemaphoreType.DMA((3, GROUPS)),
+            pltpu.SemaphoreType.DMA((3, GROUPS)),
         ],
         compiler_params=pltpu.CompilerParams(
             vmem_limit_bytes=60 * 2**20, collective_id=0, has_side_effects=True

time: 112 us -> 107 us (0.955)
  Pallas kernels: 110 us -> 106 us
    pallas_call x1, Pallas kernels: 110 us -> 106 us  [on_device(): pl.pallas_call(torus_kernel, out_shape=jax.ShapeDtypeStruct((2 * QT, D),...]
where the time goes in v8:
time: 107 us
  Pallas kernels  106 us (99%)
  local copies, waits for them, and re-layouts  1.57 us (1%)
    pallas_call x1, Pallas kernels, on_device(): pl.pallas_call(torus_kernel, out_shape=jax.ShapeDtypeStruct((2 * QT, D),...  106 us

profile of v8, /device:TPU:0, one launch (start us, length us, event | category | flops | bytes accessed | tf_op | source)
XLA Modules:
  0.0 107.2 jit_solution(8667558373222304887)
XLA Ops:
  0.0 105.6 %torus.1 = bf16[32,2048]{1,0:T(8,128)(2,1)} custom-call(s32[2]{0:T(128)} %counts_ref.1, s32[2,28]{1,0:T(2,128)} %ids_ref.1, bf16[32,2048]{1,0:T(8,128)(2,1)} %mine_ref.1, bf16[16,64,2048]{2,1,0:T(8,128)(2,1)} %k_hbm.1, bf16[16,64,2048]{2,1,0:T(8,128)(2,1)} %v_hbm.1, bf16[1024,2048]{1,0:T(8,128)(2,1)} %w_hbm.1), custom_call_target="tpu_custom_call" | custom-call | flops 40000000000 | bytes 20971520 | tf_op jit(solution)/shard_map/torus/pallas_call | solution.py:523
  105.6 1.6 %copy.8 = bf16[32,2048]{1,0:T(8,128)(2,1)} copy(bf16[32,2048]{1,0:T(8,128)(2,1)} %torus.1) | data formatting | bytes 262144

commit v9 on v8

--- a/solution.py
+++ b/solution.py
@@ -29,7 +29,7 @@
     q_ref, part_ref, near_ref, mid_ref, next_ref, late_ref, last_ref,
     part_stat, mid_stat, late_stat,
     k_ref, v_ref, w_ref, list_ref, code_ref, code_smem, score_ref, weight_ref, inverse_ref, attended_ref, sum_ref,
-    load_sem, home_sem, list_send, list_recv, w_sem, ring_send, ring_recv, tree_send, tree_recv,
+    load_sem, list_send, list_recv, w_sem, early_send, early_recv, ring_send, ring_recv, tree_send, tree_recv,
 ):
     me = lax.axis_index("dev")
     grp = lax.axis_index("grp")
@@ -50,12 +50,8 @@
         for by in line[axis]:
             pl.semaphore_signal(barrier, inc=1, device_id=line[axis][by], device_id_type=MESH)
     pl.semaphore_signal(barrier, inc=1, device_id=(1 - grp, me), device_id_type=MESH)
-    homes = [
-        pltpu.make_async_copy(mine_ref.at[:, pl.ds(g * GW, GW)], q_ref.at[g, 0, 0, 0], home_sem.at[g])
-        for g in range(GROUPS)
-    ]
-    for home in homes:
-        home.start()
+    for g in range(GROUPS):
+        q_ref[g % 3, g // 3, 0, 0, 0] = mine_ref[:, g * GW : (g + 1) * GW]
     list_len = ids_ref.shape[1]
     place = lax.broadcasted_iota(jnp.int32, (2, list_len), 1)
     row = lax.broadcasted_iota(jnp.int32, (2, list_len), 0)
@@ -66,68 +62,72 @@
 
     whole, lower, upper = (0, 2 * QT), (0, QT), (QT, QT)
     both = ((0, 1, 3, lower), (1, 3, 1, upper))
-    straight = both + ((2, 2, 2, whole),)
-
-    def sends(stage):
-        return both if stage == 2 else straight
-
     def order_of(g):
         return ORDERS[g % 3]
 
-    def ring_block(g, stage, at, rows):
-        spot = [pl.ds(0, SIDE) if n < stage else at if n == stage else 0 for n in range(3)]
-        return q_ref.at[g, spot[0], spot[1], spot[2], pl.ds(*rows), :]
-
-    def ring_own(g, stage, kind, by, at):
-        source = ring_block(g, stage, 0, whole) if stage else mine_ref.at[:, pl.ds(g * GW, GW)]
-        return pltpu.make_async_remote_copy(
-            src_ref=source,
-            dst_ref=ring_block(g, stage, at, whole),
-            send_sem=ring_send.at[g, stage],
-            recv_sem=ring_recv.at[g, stage + kind if stage == 2 else stage],
-            device_id=line[order_of(g)[stage]][by],
-            device_id_type=MESH,
-        )
-
-    def ring_pass(g, stage, kind, by, at, rows):
-        return pltpu.make_async_remote_copy(
-            src_ref=ring_block(g, stage, at, rows),
-            dst_ref=ring_block(g, stage, 2, rows),
-            send_sem=ring_send.at[g, stage],
-            recv_sem=ring_recv.at[g, 4],
-            device_id=line[order_of(g)[stage]][by],
-            device_id_type=MESH,
-        )
-
-    def ring_start(phase, stage):
+    def taken(ref, sem):
+        pltpu.make_async_copy(ref, ref, sem).wait()
+
+    def early_part(step, k, at):
+        count = len(range(k, GROUPS, 3))
+        if step == 0:
+            return q_ref.at[k, pl.ds(0, count), at, 0, 0]
+        which = pl.ds(0, 1) if step == 1 else pl.ds(1, count - 1)
+        return q_ref.at[k, which, :, at, 0]
+
+    def early_start(step):
+        for k in range(3):
+            for by in range(1, SIDE):
+                pltpu.make_async_remote_copy(
+                    src_ref=early_part(step, k, 0),
+                    dst_ref=early_part(step, k, SIDE - by),
+                    send_sem=early_send.at[k, step],
+                    recv_sem=early_recv.at[k, step],
+                    device_id=line[ORDERS[k][min(step, 1)]][by],
+                    device_id_type=MESH,
+                ).start()
+
+    def early_end(step, sem):
+        for k in range(3):
+            taken(early_part(step, k, pl.ds(1, 3)), sem.at[k, step])
+
+    def ring_block(g, at, rows):
+        return q_ref.at[g % 3, g // 3, :, :, at, pl.ds(*rows), :]
+
+    def ring_start(phase):
         for g in PHASES[phase]:
-            for kind, by, at, rows in sends(stage):
-                ring_own(g, stage, kind, by, at).start()
-
-    def ring_forward(phase, stage):
+            for kind, by, at, rows in both:
+                pltpu.make_async_remote_copy(
+                    src_ref=ring_block(g, 0, whole),
+                    dst_ref=ring_block(g, at, whole),
+                    send_sem=ring_send.at[g],
+                    recv_sem=ring_recv.at[g, kind],
+                    device_id=line[order_of(g)[2]][by],
+                    device_id_type=MESH,
+                ).start()
+
+    def ring_forward(phase):
         for kind, by, at, rows in both:
             for g in PHASES[phase]:
-                taken(ring_block(g, stage, at, whole), ring_recv.at[g, stage + kind])
-                ring_pass(g, stage, kind, by, at, rows).start()
-
-    def taken(ref, sem):
-        pltpu.make_async_copy(ref, ref, sem).wait()
-
-    def ring_all(g, stage):
-        spot = [pl.ds(0, SIDE) if n < stage else pl.ds(1, 3) if n == stage else 0 for n in range(3)]
-        return q_ref.at[g, spot[0], spot[1], spot[2]]
-
-    def ring_end(phase, stage):
+                taken(ring_block(g, at, whole), ring_recv.at[g, kind])
+                pltpu.make_async_remote_copy(
+                    src_ref=ring_block(g, at, rows),
+                    dst_ref=ring_block(g, 2, rows),
+                    send_sem=ring_send.at[g],
+                    recv_sem=ring_recv.at[g, 2],
+                    device_id=line[order_of(g)[2]][by],
+                    device_id_type=MESH,
+                ).start()
+
+    def ring_end(phase):
         for g in PHASES[phase]:
-            if stage == 2:
-                taken(ring_block(g, stage, 2, whole), ring_recv.at[g, 4])
-            else:
-                taken(ring_all(g, stage), ring_recv.at[g, stage])
+            taken(ring_block(g, 2, whole), ring_recv.at[g, 2])
 
     def ring_sent():
+        for step in range(3):
+            early_end(step, early_send)
         for g in range(GROUPS):
-            for stage in range(3):
-                taken(ring_all(g, stage), ring_send.at[g, stage])
+            taken(q_ref.at[g % 3, g // 3, :, :, pl.ds(1, 3)], ring_send.at[g])
 
     def list_copy(stage, by):
         order = ("x", "y", "z")
@@ -173,18 +173,17 @@
     )
 
     list_start(0)
-    ring_start(0, 0)
+    early_start(0)
     part_stat[...] = jnp.zeros(part_stat.shape, jnp.float32)
-    for home in homes:
-        home.wait()
     list_end(0)
     list_start(1)
-    ring_end(0, 0)
-    ring_start(0, 1)
+    early_end(0, early_recv)
+    early_start(1)
     list_end(1)
     list_start(2)
-    ring_end(0, 1)
-    ring_start(0, 2)
+    early_end(1, early_recv)
+    ring_start(0)
+    early_start(2)
     list_end(2)
     firsts, lasts = [], []
     for n in range(2):
@@ -267,7 +266,7 @@
         which, first, second = passages(told(phase, b, n, g))
         cols = slice(g * GW, (g + 1) * GW)
         spot = place(phase, b, n)
-        q = jnp.where(which > 0, q_ref[(g, *spot, slice(QT, 2 * QT))], q_ref[(g, *spot, slice(0, QT))])
+        q = jnp.where(which > 0, q_ref[(g % 3, g // 3, *spot, slice(QT, 2 * QT))], q_ref[(g % 3, g // 3, *spot, slice(0, QT))])
         lhs = jnp.concatenate([q] * GH, axis=0) * diag
         k = jnp.concatenate([k_ref[first, :, cols], k_ref[second, :, cols]], axis=0)
         score_ref[at] = lax.dot_general(lhs, k, (((1,), (1,)), ((), ())), preferred_element_type=jnp.float32)
@@ -471,27 +470,17 @@
     run(
         0,
         {
-            1: [(ring_forward, 0, 2), (ring_start, 1, 0)],
-            5: [(ring_end, 1, 0), (ring_start, 1, 1)],
-            9: [(ring_end, 0, 2)],
-            10: [(ring_end, 1, 1), (ring_start, 1, 2)],
+            1: [(ring_forward, 0)],
+            4: [(early_end, 2, early_recv), (ring_start, 1)],
+            9: [(ring_end, 0)],
+            13: [(ring_forward, 1), (ring_start, 2)],
         },
     )
     send(0, 2, 1, 3)
-    run(
-        1,
-        {
-            0: [(ring_start, 2, 0)],
-            1: [(ring_forward, 1, 2)],
-            4: [(ring_end, 2, 0), (ring_start, 2, 1)],
-            8: [(ring_end, 2, 1), (ring_start, 2, 2)],
-            9: [(ring_end, 1, 2)],
-            14: [(ring_forward, 2, 2)],
-        },
-    )
+    run(1, {6: [(ring_forward, 2)], 9: [(ring_end, 1)]})
     send(1, 2, 1, 3)
     each(merge_one, 0)
-    ring_end(2, 2)
+    ring_end(2)
     run(2, {3: [(send, 2, 1)], 7: [(send, 2, 2)], 11: [(send, 2, 3)]})
     each(merge_two, 0)
     each(merge_one, 1)
@@ -514,7 +503,7 @@
 
 
 def on_device(queries, keys, values, counts, passage_ids, out_weight):
-    blocks = [pltpu.VMEM((GROUPS, SIDE, SIDE, SIDE, 2 * QT, GW), jnp.bfloat16)]
+    blocks = [pltpu.VMEM((3, 3, SIDE, SIDE, SIDE, 2 * QT, GW), jnp.bfloat16)]
     for count in (SIDE * SIDE, 2 * SIDE, 2):
         for lead in (SIDE, SIDE - 1):
             blocks.append(pltpu.VMEM((GROUPS, lead, count + 2, QT, GW), jnp.bfloat16))
@@ -541,12 +530,13 @@
             pltpu.VMEM((2 * QT, D), jnp.bfloat16),
             pltpu.VMEM((2 * QT, D), jnp.float32),
             pltpu.SemaphoreType.DMA((4,)),
-            pltpu.SemaphoreType.DMA((GROUPS,)),
             pltpu.SemaphoreType.DMA((3, SIDE)),
             pltpu.SemaphoreType.DMA((3, SIDE)),
             pltpu.SemaphoreType.DMA((2,)),
+            pltpu.SemaphoreType.DMA((3, 3)),
+            pltpu.SemaphoreType.DMA((3, 3)),
+            pltpu.SemaphoreType.DMA((GROUPS,)),
             pltpu.SemaphoreType.DMA((GROUPS, 3)),
-            pltpu.SemaphoreType.DMA((GROUPS, 5)),
             pltpu.SemaphoreType.DMA((3, GROUPS)),
             pltpu.SemaphoreType.DMA((3, GROUPS)),
         ],

time: 107 us -> 99.5 us (0.930)
  Pallas kernels: 106 us -> 97.1 us
    pallas_call x1, Pallas kernels: 106 us -> 97.1 us  [on_device(): pl.pallas_call(torus_kernel, out_shape=jax.ShapeDtypeStruct((2 * QT, D),...]
where the time goes in v9:
time: 99.5 us; the launch traced here: 98.7 us
  Pallas kernels  97.1 us (98%)
  local copies, waits for them, and re-layouts  1.57 us (2%)
    pallas_call x1, Pallas kernels, on_device(): pl.pallas_call(torus_kernel, out_shape=jax.ShapeDtypeStruct((2 * QT, D),...  97.1 us

profile of v9, /device:TPU:0, one launch (start us, length us, event | category | flops | bytes accessed | tf_op | source)
XLA Modules:
  0.0 98.7 jit_solution(5201437082252169992)
XLA Ops:
  0.0 97.1 %torus.1 = bf16[32,2048]{1,0:T(8,128)(2,1)} custom-call(s32[2]{0:T(128)} %counts_ref.1, s32[2,28]{1,0:T(2,128)} %ids_ref.1, bf16[32,2048]{1,0:T(8,128)(2,1)} %mine_ref.1, bf16[16,64,2048]{2,1,0:T(8,128)(2,1)} %k_hbm.1, bf16[16,64,2048]{2,1,0:T(8,128)(2,1)} %v_hbm.1, bf16[1024,2048]{1,0:T(8,128)(2,1)} %w_hbm.1), custom_call_target="tpu_custom_call" | custom-call | flops 40000000000 | bytes 20971520 | tf_op jit(solution)/shard_map/torus/pallas_call | solution.py:512
  97.1 1.6 %copy.8 = bf16[32,2048]{1,0:T(8,128)(2,1)} copy(bf16[32,2048]{1,0:T(8,128)(2,1)} %torus.1) | data formatting | bytes 262144

commit v10 on v9

--- a/solution.py
+++ b/solution.py
@@ -19,6 +19,7 @@
 PHASES = ((0, 1, 2), (3, 4, 5), (6, 7))
 BATCH = 4
 
+GRAY = (0, 1, 3, 2)
 DEAD = -1e30
 ORDERS = (("x", "y", "z"), ("y", "z", "x"), ("z", "x", "y"))
 MESH = pl.DeviceIdType.MESH
@@ -211,11 +212,13 @@
 
     trees = ((part_ref, near_ref), (mid_ref, next_ref), (late_ref, last_ref))
 
-    def tree_start(stage, g, by):
-        source, target = trees[stage]
+    def tree_start(stage, g, by, rows=None):
+        source, target = (ref.at[g, at] for ref, at in zip(trees[stage], (by, by - 1)))
+        if rows is not None:
+            source, target = source.at[pl.ds(*rows)], target.at[pl.ds(*rows)]
         pltpu.make_async_remote_copy(
-            src_ref=source.at[g, by],
-            dst_ref=target.at[g, by - 1],
+            src_ref=source,
+            dst_ref=target,
             send_sem=tree_send.at[stage, g],
             recv_sem=tree_recv.at[stage, g],
             device_id=line[order_of(g)[stage]][by],
@@ -248,8 +251,10 @@
             return quarter, n, turn + (turn >> 1) * (1 - 2 * (turn & 1))
         return (turn + 1) & 3, quarter, n
 
-    def block_of(g, spot):
-        return g, spot[0], spot[1] * SIDE + spot[2]
+    def block_of(g, phase, b, n):
+        if phase < 2:
+            return g, b & 3, (b >> 2) * SIDE + n
+        return g, ((b >> 2) + 1) & 3, GRAY[n] * SIDE + (b & 3)
 
     def told(phase, b, n, g):
         return code_smem[sum(at * stride[axis] for axis, at in zip(order_of(g), place(phase, b, n))), 0, 0]
@@ -306,7 +311,7 @@
             lanes = slice(t * LANE, (t + 1) * LANE)
             a, c = (slice((2 * t + e) * QT, (2 * t + e + 1) * QT) for e in (0, 1))
             part = jnp.where(near, full[a, lanes], full[c, lanes]) * inverse_ref[at, :, lanes]
-            part_ref[(*block_of(g, place(phase, b, n)), slice(None), lanes)] = part.astype(jnp.bfloat16)
+            part_ref[(*block_of(g, phase, b, n), slice(None), lanes)] = part.astype(jnp.bfloat16)
 
     def pack_open(phase, b):
         first, second, third = place(phase, b, 0)
@@ -382,9 +387,10 @@
         ]
 
         def body(j, carry):
-            second, third = j >> 2, j & 3
+            second, turn = j & 3, j >> 2
+            third = turn + (turn >> 1) * (1 - 2 * (turn & 1))
             blocks = [part_ref[g, 0, j]] + [near_ref[g, d - 1, j] for d in range(1, SIDE)]
-            turned = [pltpu.roll(share, (LANE - GH * j) & (LANE - 1), 1) for share in shares]
+            turned = [pltpu.roll(share, (LANE - GH * (second * SIDE + third)) & (LANE - 1), 1) for share in shares]
             for t in range(GW // LANE):
                 totals = [jnp.zeros((QT, LANE), jnp.float32)] * 2
                 for d in range(SIDE):
@@ -447,6 +453,13 @@
                 put_stat(part_ref, g, by, part_stat[g, by])
                 tree_start(0, g, by)
 
+    def send_turn(phase, turn):
+        for by in (2, 1, 3):
+            for g in PHASES[phase]:
+                if turn == SIDE - 1:
+                    put_stat(part_ref, g, by, part_stat[g, by])
+                tree_start(0, g, by, (turn * SIDE, SIDE + 2 if turn == SIDE - 1 else SIDE))
+
     def run(phase, beside):
         prepare(phase)
 
@@ -477,8 +490,17 @@
         },
     )
     send(0, 2, 1, 3)
-    run(1, {6: [(ring_forward, 2)], 9: [(ring_end, 1)]})
-    send(1, 2, 1, 3)
+    run(
+        1,
+        {
+            3: [(send_turn, 1, 0)],
+            6: [(ring_forward, 2)],
+            7: [(send_turn, 1, 1)],
+            9: [(ring_end, 1)],
+            11: [(send_turn, 1, 2)],
+        },
+    )
+    send_turn(1, 3)
     each(merge_one, 0)
     ring_end(2)
     run(2, {3: [(send, 2, 1)], 7: [(send, 2, 2)], 11: [(send, 2, 3)]})

time: 99.5 us -> 101 us (1.015)
  Pallas kernels: 97.1 us -> 99.1 us
    pallas_call x1, Pallas kernels: 97.1 us -> 99.1 us  [on_device(): pl.pallas_call(torus_kernel, out_shape=jax.ShapeDtypeStruct((2 * QT, D),...]
where the time goes in v10:
time: 101 us
  Pallas kernels  99.1 us (98%)
  local copies, waits for them, and re-layouts  1.57 us (2%)
    pallas_call x1, Pallas kernels, on_device(): pl.pallas_call(torus_kernel, out_shape=jax.ShapeDtypeStruct((2 * QT, D),...  99.1 us

profile of v10, /device:TPU:0, one launch (start us, length us, event | category | flops | bytes accessed | tf_op | source)
XLA Modules:
  0.0 100.7 jit_solution(17268128854198776487)
XLA Ops:
  0.0 99.1 %torus.1 = bf16[32,2048]{1,0:T(8,128)(2,1)} custom-call(s32[2]{0:T(128)} %counts_ref.1, s32[2,28]{1,0:T(2,128)} %ids_ref.1, bf16[32,2048]{1,0:T(8,128)(2,1)} %mine_ref.1, bf16[16,64,2048]{2,1,0:T(8,128)(2,1)} %k_hbm.1, bf16[16,64,2048]{2,1,0:T(8,128)(2,1)} %v_hbm.1, bf16[1024,2048]{1,0:T(8,128)(2,1)} %w_hbm.1), custom_call_target="tpu_custom_call" | custom-call | flops 40000000000 | bytes 20971520 | tf_op jit(solution)/shard_map/torus/pallas_call | solution.py:534
  99.1 1.6 %copy.8 = bf16[32,2048]{1,0:T(8,128)(2,1)} copy(bf16[32,2048]{1,0:T(8,128)(2,1)} %torus.1) | data formatting | bytes 262144

commit v11 on v9

--- a/solution.py
+++ b/solution.py
@@ -183,7 +183,6 @@
     list_start(2)
     early_end(1, early_recv)
     ring_start(0)
-    early_start(2)
     list_end(2)
     firsts, lasts = [], []
     for n in range(2):
@@ -197,8 +196,6 @@
     code_ref[...] = jnp.broadcast_to(code, (OWNERS, LANE)).reshape(OWNERS, 1, LANE)
     code_move = pltpu.make_async_copy(code_ref, code_smem, load_sem.at[3])
     code_move.start()
-    w_home.start()
-    w_give.start()
     for load in loads:
         load.wait()
     code_move.wait()
@@ -467,17 +464,21 @@
         for g in PHASES[phase]:
             merge(g)
 
+    def weights_start():
+        w_home.start()
+        w_give.start()
+
     run(
         0,
         {
-            1: [(ring_forward, 0)],
-            4: [(early_end, 2, early_recv), (ring_start, 1)],
+            1: [(ring_forward, 0), (early_start, 2)],
+            6: [(early_end, 2, early_recv), (ring_start, 1)],
             9: [(ring_end, 0)],
-            13: [(ring_forward, 1), (ring_start, 2)],
+            14: [(ring_forward, 1), (ring_start, 2)],
         },
     )
     send(0, 2, 1, 3)
-    run(1, {6: [(ring_forward, 2)], 9: [(ring_end, 1)]})
+    run(1, {6: [(ring_forward, 2)], 9: [(ring_end, 1)], 10: [(weights_start,)]})
     send(1, 2, 1, 3)
     each(merge_one, 0)
     ring_end(2)

time: 99.5 us -> 103 us (1.035)
  Pallas kernels: 97.1 us -> 101 us
    pallas_call x1, Pallas kernels: 97.1 us -> 101 us  [on_device(): pl.pallas_call(torus_kernel, out_shape=jax.ShapeDtypeStruct((2 * QT, D),...]
where the time goes in v11:
time: 103 us
  Pallas kernels  101 us (98%)
  local copies, waits for them, and re-layouts  1.57 us (2%)
    pallas_call x1, Pallas kernels, on_device(): pl.pallas_call(torus_kernel, out_shape=jax.ShapeDtypeStruct((2 * QT, D),...  101 us

profile of v11, /device:TPU:0, one launch (start us, length us, event | category | flops | bytes accessed | tf_op | source)
XLA Modules:
  0.0 102.7 jit_solution(6088057996154585193)
XLA Ops:
  0.0 101.1 %torus.1 = bf16[32,2048]{1,0:T(8,128)(2,1)} custom-call(s32[2]{0:T(128)} %counts_ref.1, s32[2,28]{1,0:T(2,128)} %ids_ref.1, bf16[32,2048]{1,0:T(8,128)(2,1)} %mine_ref.1, bf16[16,64,2048]{2,1,0:T(8,128)(2,1)} %k_hbm.1, bf16[16,64,2048]{2,1,0:T(8,128)(2,1)} %v_hbm.1, bf16[1024,2048]{1,0:T(8,128)(2,1)} %w_hbm.1), custom_call_target="tpu_custom_call" | custom-call | flops 40000000000 | bytes 20971520 | tf_op jit(solution)/shard_map/torus/pallas_call | solution.py:513
  101.1 1.6 %copy.8 = bf16[32,2048]{1,0:T(8,128)(2,1)} copy(bf16[32,2048]{1,0:T(8,128)(2,1)} %torus.1) | data formatting | bytes 262144
